TPU v7x, 32 devices: a whole 2x2x4 slice. The times are simulated.
32 devices in a mesh: dp: 16 (over z, x, core), tensor: 2 (over y).
Axes of the slice: x: 2, y: 2, z: 4, core: 2. Of those that a mesh axis runs over, the one named last changes fastest.
Arguments:
- residual: float32 [4096, 1024], P(('dp', 'tensor')), may hold values from -6 to 6
- out_grad: float32 [4096, 1024], P(('dp', 'tensor')), may hold values from -6 to 6
- doc_lengths: int32 [16, 4], P('dp'), may hold values from 0 to 256, as said below
- mixer_weight: float32 [1024, 3840], P('dp', 'tensor'), may hold values from -0.1875 to 0.1875
- mixer_first: float32 [1024, 3840], P('dp', 'tensor'), may hold values from -40 to 40
- mixer_second: float32 [1024, 3840], P('dp', 'tensor'), may hold values from 102.4 to 1638.4
- scan_weight: float32 [1024, 280], P('dp'), may hold values from -0.1875 to 0.1875
- scan_first: float32 [1024, 280], P('dp'), may hold values from -40 to 40
- scan_second: float32 [1024, 280], P('dp'), may hold values from 102.4 to 1638.4
- merge_weight: float32 [2048, 1024], P('tensor', 'dp'), may hold values from -0.25 to 0.25
- merge_first: float32 [2048, 1024], P('tensor', 'dp'), may hold values from -40 to 40
- merge_second: float32 [2048, 1024], P('tensor', 'dp'), may hold values from 102.4 to 1638.4
- hidden_weight: float32 [1024, 4096], P('dp', 'tensor'), may hold values from -0.1875 to 0.1875
- hidden_first: float32 [1024, 4096], P('dp', 'tensor'), may hold values from -40 to 40
- hidden_second: float32 [1024, 4096], P('dp', 'tensor'), may hold values from 102.4 to 1638.4
- down_weight: float32 [2048, 1024], P('tensor', 'dp'), may hold values from -0.125 to 0.125
- down_first: float32 [2048, 1024], P('tensor', 'dp'), may hold values from -40 to 40
- down_second: float32 [2048, 1024], P('tensor', 'dp'), may hold values from 102.4 to 1638.4
- head_params: float32 [24, 323], P('tensor'), may hold values from -4 to 1.5, as said below
- head_first: float32 [24, 323], P('tensor'), may hold values from -40 to 40
- head_second: float32 [24, 323], P('tensor'), may hold values from 102.4 to 1638.4
- shared_params: float32 [3328], replicated, may hold values from -1.5 to 1.5, as said below
- shared_first: float32 [3328], replicated, may hold values from -40 to 40
- shared_second: float32 [3328], replicated, may hold values from 102.4 to 1638.4
Outputs:
- block_out: float32 [4096, 1024], P(('dp', 'tensor'))
- input_grad: float32 [4096, 1024], P(('dp', 'tensor'))
- mixer_momentum: float32 [1024, 3840], P('dp', 'tensor')
- mixer_squares: float32 [1024, 3840], P('dp', 'tensor')
- mixer_updated: float32 [1024, 3840], P('dp', 'tensor')
- scan_momentum: float32 [1024, 280], P('dp')
- scan_squares: float32 [1024, 280], P('dp')
- scan_updated: float32 [1024, 280], P('dp')
- merge_momentum: float32 [2048, 1024], P('tensor', 'dp')
- merge_squares: float32 [2048, 1024], P('tensor', 'dp')
- merge_updated: float32 [2048, 1024], P('tensor', 'dp')
- hidden_momentum: float32 [1024, 4096], P('dp', 'tensor')
- hidden_squares: float32 [1024, 4096], P('dp', 'tensor')
- hidden_updated: float32 [1024, 4096], P('dp', 'tensor')
- down_momentum: float32 [2048, 1024], P('tensor', 'dp')
- down_squares: float32 [2048, 1024], P('tensor', 'dp')
- down_updated: float32 [2048, 1024], P('tensor', 'dp')
- head_momentum: float32 [24, 323], P('tensor')
- head_squares: float32 [24, 323], P('tensor')
- head_updated: float32 [24, 323], P('tensor')
- shared_momentum: float32 [3328], replicated
- shared_squares: float32 [3328], replicated
- shared_updated: float32 [3328], replicated
Inputs may be any that keep to these rules, and one draw needn't show every extreme that they name: `doc_lengths`: each row lists the lengths of the documents of one group in order and sums to 256; zeros are empty slots. The first document of each row is longer than half of 256; one row holds a single document of 256 tokens. `head_params`: columns below 256: convolution taps; next 64: biases; then a_log, skip, dt_bias. `shared_params`: gains first, then taps, then biases.
All inputs are finite; a program needn't handle non-finite values.
Results may differ from a plain program's by a relative error of at most 0.012.
The roundings to bfloat16 on the way count: a program that leaves them out, or rounds other values in their place, can miss the bound.
Values may be sent and summed in bfloat16 or wider, within the bound.
No kernel may reach another device: no remote copies, remote signals or barrier semaphores. Data moves between devices by JAX's collectives and lax.ppermute only.
A program may use at most 128 MiB of HBM per device.

v0:
```python
import jax
import jax.numpy as jnp
from jax import lax
from jax.experimental import pallas as pl
from jax.experimental.pallas import tpu as pltpu
from jax.sharding import PartitionSpec as P

D = 1024
HEADS_M = 24
HEAD_M = 64
STATE = 128
CONV = 4
HEADS_Q = 8
HEADS_KV = 2
HEAD_A = 64
STEP = 10
CORES = 2


EPS = 1e-05
THETA = 10000.0
HIGH = lax.Precision.HIGHEST


def scaled_norm(values, gain):
    return values * lax.rsqrt(jnp.mean(values * values, axis=-1, keepdims=True) + EPS) * gain


def norm_scale(values):
    return lax.rsqrt(jnp.mean(values * values, axis=-1, keepdims=True) + EPS)


def norm_back(values, gain, grad):
    scale = norm_scale(values)
    scaled = grad * gain
    inner = jnp.mean(values * scaled, axis=-1, keepdims=True)
    return scale * scaled - values * (scale * scale * scale * inner)


def doc_index(lens, count):
    place = jnp.arange(count, dtype=jnp.int32)
    ends = jnp.cumsum(lens)
    after = place[:, None] >= ends[None, :]
    seg = jnp.sum(after.astype(jnp.int32), axis=1)
    start = jnp.sum(jnp.where(after, lens[None, :], 0), axis=1)
    return (seg, place - start)


HEADS = HEADS_M // 2
WIDTH = HEADS * HEAD_M
QCOLS = HEADS_Q // 2 * HEAD_A
LANES = 128
RATE_COL = (CONV + 1) * HEAD_M
SKIP_COL = RATE_COL + 1
BIAS_COL = RATE_COL + 2


def exact_dot(left, right, dims=((1,), (0,))):
    return lax.dot_general(
        left, right, (dims, ((), ())), precision=HIGH, preferred_element_type=jnp.float32
    )


def low_dot(left, right, dims=((1,), (0,))):
    return lax.dot_general(
        left.astype(jnp.bfloat16),
        right.astype(jnp.bfloat16),
        (dims, ((), ())),
        preferred_element_type=jnp.float32,
    )


ROWS = ((0,), (0,))
COLS = ((1,), (1,))


def lane_of(shape):
    return lax.broadcasted_iota(jnp.int32, shape, 1)


def shifted(values, pos, shift):
    return jnp.where(pos >= shift, pltpu.roll(values, shift, 0), 0.0)


def conv_forward(values, rows, pos):
    total = rows[CONV : CONV + 1] + rows[CONV - 1 : CONV] * values
    for shift in range(1, CONV):
        tap = rows[CONV - 1 - shift : CONV - shift]
        total = total + tap * shifted(values, pos, shift)
    return total


def conv_backward(grad, values, rows, pos):
    length = values.shape[0]
    back = rows[CONV - 1 : CONV] * grad
    taps = [jnp.sum(grad * values, axis=0, keepdims=True)]
    for shift in range(1, CONV):
        tap = rows[CONV - 1 - shift : CONV - shift]
        kept = jnp.where(pos >= shift, grad, 0.0)
        back = back + tap * pltpu.roll(kept, length - shift, 0)
        taps.append(jnp.sum(kept * pltpu.roll(values, shift, 0), axis=0, keepdims=True))
    return back, taps[::-1] + [jnp.sum(grad, axis=0, keepdims=True)]


def swap_pairs(values):
    first = lane_of(values.shape) % HEAD_A < HEAD_A // 2
    half = HEAD_A // 2
    return jnp.where(first, pltpu.roll(values, LANES - half, 1), pltpu.roll(values, half, 1))


def turn(values, cosine, sine):
    return values * cosine + swap_pairs(values) * sine


def turn_back(values, cosine, sine):
    return values * cosine + swap_pairs(values * sine)


def half_lanes(values, which):
    mine = lane_of(values.shape) // HEAD_A == which
    return jnp.where(mine, values, jnp.zeros_like(values))


def column_to_lanes(column):
    shape = (column.shape[0], LANES)
    row = lax.broadcasted_iota(jnp.int32, shape, 0)
    mine = (row == lane_of(shape)) & (row < HEADS)
    return jnp.sum(jnp.where(mine, column, 0.0), axis=0, keepdims=True)


def conv_rows(heads_ref):
    tiles = [heads_ref[:, j * LANES : (j + 1) * LANES] for j in range(3)]
    rolled = [pltpu.roll(tile, HEAD_M, 1) for tile in tiles]
    left = lane_of((1, LANES)) < HEAD_M
    rows = []
    for k in range(CONV + 1):
        kinds = (tiles[k // 2], rolled[k // 2])
        even, odd = kinds[k % 2], kinds[1 - k % 2]
        pieces = [
            jnp.where(left, even[h : h + 1], odd[h + 1 : h + 2]) for h in range(0, HEADS, 2)
        ]
        rows.append(jnp.concatenate(pieces, axis=1))
    skip = heads_ref[:, SKIP_COL : SKIP_COL + 1]
    pieces = [jnp.where(left, skip[h : h + 1], skip[h + 1 : h + 2]) for h in range(0, HEADS, 2)]
    rows.append(jnp.concatenate(pieces, axis=1))
    return jnp.concatenate(rows + [jnp.zeros((2, WIDTH), jnp.float32)], axis=0)


def head_rows(rows, dlog, dbias):
    left = lane_of((1, LANES)) < HEAD_M
    lane = lane_of((1, LANES))
    out = []
    for i in range(HEADS // 2):
        tile = rows[:, i * LANES : (i + 1) * LANES]
        kinds = (tile, pltpu.roll(tile, HEAD_M, 1))
        for which in range(2):
            h = 2 * i + which
            piece = [kinds[(which + k) % 2][k : k + 1] for k in range(CONV + 1)]
            dskip = jnp.sum(
                half_lanes(tile[CONV + 1 : CONV + 2], which), axis=1, keepdims=True
            )
            last = jnp.where(lane == HEAD_M, dlog[:, h : h + 1], 0.0)
            last = jnp.where(lane == HEAD_M + 1, dskip, last)
            last = jnp.where(lane == HEAD_M + 2, dbias[:, h : h + 1], last)
            tiles = [
                jnp.where(left, piece[0], piece[1]),
                jnp.where(left, piece[2], piece[3]),
                jnp.where(left, piece[4], last),
            ]
            out.append(jnp.concatenate(tiles, axis=1))
    out.append(jnp.zeros((16 - HEADS, 3 * LANES), jnp.float32))
    return jnp.concatenate(out, axis=0)


def documents(lens_ref, place):
    seg, start, end = jnp.zeros_like(place), jnp.zeros_like(place), 0
    for k in range(lens_ref.shape[0]):
        end = end + lens_ref[k]
        after = place >= end
        seg = seg + jnp.where(after, 1, 0)
        start = start + jnp.where(after, lens_ref[k], 0)
    return seg, place - start


def split_rows(values, tidx, mine_ref, theirs_ref):
    half = values.shape[0] // 2
    upper, lower = values[:half], values[half:]
    mine_ref[...] = jnp.where(tidx == 0, upper, lower)
    theirs_ref[...] = jnp.where(tidx == 0, lower, upper).astype(theirs_ref.dtype)


def split_columns(left, right, core, keep_ref, give_ref):
    keep_ref[...] = jnp.where(core == 0, left, right)
    give_ref[...] = jnp.where(core == 0, right, left)


def mixer_parts(tidx_ref, lens_ref, p_ref, heads_ref, bc_ref):
    length = p_ref.shape[0]
    base = 2 * WIDTH + QCOLS + 2 * HEAD_A
    conv = conv_rows(heads_ref)
    bc = bc_ref[...]
    row = lax.broadcasted_iota(jnp.int32, (length, length), 0)
    column = lax.broadcasted_iota(jnp.int32, (length, length), 1)
    seg, pos = documents(lens_ref, lax.broadcasted_iota(jnp.int32, (length, 1), 0))
    seg_across, _ = documents(lens_ref, lax.broadcasted_iota(jnp.int32, (1, length), 1))
    same = (seg == seg_across) & (row >= column)
    wide = p_ref[:, WIDTH : 2 * WIDTH].astype(jnp.float32)
    chans_pre = conv_forward(wide, conv, pos)
    chans_sig = jax.nn.sigmoid(chans_pre)
    states = p_ref[:, base : base + 2 * STATE].astype(jnp.float32)
    states_pre = conv_forward(states, bc, pos)
    states_sig = jax.nn.sigmoid(states_pre)
    raw = p_ref[:, base + 2 * STATE : base + 2 * STATE + LANES].astype(jnp.float32)
    i = lax.broadcasted_iota(jnp.int32, (LANES, LANES), 0)
    j = lane_of((LANES, LANES))
    sel = ((i == HEADS * tidx_ref[0] + j) & (j < HEADS)).astype(jnp.float32)
    i = lax.broadcasted_iota(jnp.int32, (LANES, WIDTH), 0)
    spread = (i == lane_of((LANES, WIDTH)) // HEAD_M).astype(jnp.float32)
    rates = column_to_lanes(jnp.exp(heads_ref[:, RATE_COL : RATE_COL + 1]))
    bias = column_to_lanes(heads_ref[:, BIAS_COL : BIAS_COL + 1])
    step_pre = exact_dot(raw, sel) + bias
    steps = jnp.maximum(step_pre, 0.0) + jnp.log1p(jnp.exp(-jnp.abs(step_pre)))
    before = (row >= column).astype(jnp.float32)
    cum = exact_dot(before, -rates * steps)
    steps_wide = exact_dot(steps, spread)
    chans = chans_pre * chans_sig
    states_out = states_pre * states_sig
    in_state, out_state = states_out[:, :STATE], states_out[:, STATE:]
    inner = jnp.where(same, exact_dot(out_state, in_state, COLS), 0.0)
    return dict(
        pos=pos, wide=wide, chans_pre=chans_pre, chans_sig=chans_sig, chans=chans,
        states=states, states_pre=states_pre, states_sig=states_sig, in_state=in_state,
        out_state=out_state, step_pre=step_pre, steps=steps, rates=rates, before=before,
        cum=cum, cum_t=cum.T, same=same, steps_wide=steps_wide, inner=inner, conv=conv, bc=bc,
        sel=sel, spread=spread, weighted=(steps_wide * chans).astype(jnp.bfloat16),
    )


def decay_of(parts, head):
    gap = parts["cum"][:, head : head + 1] - parts["cum_t"][head : head + 1, :]
    return jnp.exp(jnp.minimum(gap, 0.0))


def attention_parts(p_ref, cos_ref, sin_ref):
    cosine, sine = cos_ref[...], sin_ref[...]
    pairs = []
    for i in range(QCOLS // LANES):
        a = 2 * WIDTH + i * LANES
        query = turn(p_ref[:, a : a + LANES].astype(jnp.float32), cosine, sine)
        pairs.append((query * HEAD_A ** (-0.5)).astype(jnp.bfloat16))
    a = 2 * WIDTH + QCOLS
    both = p_ref[:, a : a + LANES].astype(jnp.float32)
    key = half_lanes(turn(both, cosine, sine), 0)
    value = half_lanes(both, 1)
    keys = (key.astype(jnp.bfloat16), pltpu.roll(key, HEAD_A, 1).astype(jnp.bfloat16))
    values = (pltpu.roll(value, HEAD_A, 1).astype(jnp.bfloat16), value.astype(jnp.bfloat16))
    return pairs, keys, values


def attention_probs(query, key, same):
    scores = jnp.where(same, low_dot(query, key, COLS), -1e30)
    top = jnp.max(scores, axis=1, keepdims=True)
    raised = jnp.exp(scores - top)
    return raised / jnp.sum(raised, axis=1, keepdims=True)


def forward_kernel(
    tidx_ref, lens_ref, p_ref, heads_ref, bc_ref, cos_ref, sin_ref, w_ref,
    cat_ref, y_ref, mine_ref, theirs_ref, keep_ref, give_ref,
):
    parts = mixer_parts(tidx_ref, lens_ref, p_ref, heads_ref, bc_ref)
    for i in range(WIDTH // LANES):
        a = i * LANES
        tile = parts["weighted"][:, a : a + LANES]
        out = jnp.zeros((p_ref.shape[0], LANES), jnp.float32)
        for which in range(2):
            mixed = decay_of(parts, 2 * i + which) * parts["inner"]
            out = out + low_dot(mixed, half_lanes(tile, which))
        y_ref[:, a : a + LANES] = out
        gate = p_ref[:, a : a + LANES].astype(jnp.float32)
        out = out + parts["conv"][CONV + 1 : CONV + 2, a : a + LANES] * parts["chans"][:, a : a + LANES]
        cat_ref[:, a : a + LANES] = (out * gate * jax.nn.sigmoid(gate)).astype(cat_ref.dtype)
    pairs, keys, values = attention_parts(p_ref, cos_ref, sin_ref)
    for i, query in enumerate(pairs):
        out = jnp.zeros((p_ref.shape[0], LANES), jnp.float32)
        for which in range(2):
            probs = attention_probs(query, keys[which], parts["same"])
            out = out + low_dot(probs, values[which])
        a = WIDTH + i * LANES
        cat_ref[:, a : a + LANES] = out.astype(cat_ref.dtype)
    cat = cat_ref[...]
    split_rows(dot_t(cat, w_ref[:, p_ref.shape[1] :]), tidx_ref[0], mine_ref, theirs_ref)
    half = cat.shape[1] // 2
    split_columns(cat[:, :half], cat[:, half:], tidx_ref[1], keep_ref, give_ref)


def backward_kernel(
    tidx_ref, lens_ref, p_ref, heads_ref, bc_ref, cos_ref, sin_ref, y_ref, dmix_ref, w_ref,
    dp_ref, dheads_ref, dbc_ref, keep_ref, give_ref,
):
    length = p_ref.shape[0]
    low = dp_ref.dtype
    parts = mixer_parts(tidx_ref, lens_ref, p_ref, heads_ref, bc_ref)
    pos, chans = parts["pos"], parts["chans"]
    gate = p_ref[:, :WIDTH].astype(jnp.float32)
    gate_sig = jax.nn.sigmoid(gate)
    grad_all = dot(dmix_ref[...], w_ref[:, p_ref.shape[1] :])
    grad = grad_all[:, :WIDTH]
    skip = parts["conv"][CONV + 1 : CONV + 2]
    outputs = y_ref[...]
    dgate = grad * (outputs + skip * chans) * gate_sig * (1.0 + gate * (1.0 - gate_sig))
    dp_ref[:, :WIDTH] = dgate.astype(low)
    dy = grad * gate * gate_sig
    dy_low = dy.astype(jnp.bfloat16)
    dweighted = []
    dinner = jnp.zeros((length, length), jnp.float32)
    for i in range(WIDTH // LANES):
        a = i * LANES
        tile = parts["weighted"][:, a : a + LANES]
        out = jnp.zeros((length, LANES), jnp.float32)
        for which in range(2):
            decay = decay_of(parts, 2 * i + which)
            dy_half = half_lanes(dy_low[:, a : a + LANES], which)
            out = out + low_dot(decay * parts["inner"], dy_half, ROWS)
            dinner = dinner + low_dot(dy_half, tile, COLS) * decay
        dweighted.append(out)
    dweighted = jnp.concatenate(dweighted, axis=1)
    spread = parts["spread"]
    weighted = parts["weighted"].astype(jnp.float32)
    dcum = exact_dot(dy_low.astype(jnp.float32) * outputs - weighted * dweighted, spread, COLS)
    dsteps = exact_dot(dweighted * chans, spread, COLS)
    dchans = skip * dy + parts["steps_wide"] * dweighted
    drate = exact_dot(parts["before"], dcum, ROWS)
    dsteps = (dsteps - parts["rates"] * drate) * jax.nn.sigmoid(parts["step_pre"])
    dlog = jnp.sum(-parts["rates"] * parts["steps"] * drate, axis=0, keepdims=True)
    dbias = jnp.sum(dsteps, axis=0, keepdims=True)
    base = 2 * WIDTH + QCOLS + 2 * HEAD_A
    draw = exact_dot(dsteps, parts["sel"], COLS)
    dp_ref[:, base + 2 * STATE :] = draw.astype(low)

    sig, pre = parts["chans_sig"], parts["chans_pre"]
    dpre = dchans * sig * (1.0 + pre * (1.0 - sig))
    back, rows = conv_backward(dpre, parts["wide"], parts["conv"], pos)
    dp_ref[:, WIDTH : 2 * WIDTH] = back.astype(low)
    rows.append(jnp.sum(dy * chans, axis=0, keepdims=True))
    rows = jnp.concatenate(rows + [jnp.zeros((2, WIDTH), jnp.float32)], axis=0)
    dheads_ref[...] = head_rows(rows, dlog, dbias)

    dinner = jnp.where(parts["same"], dinner, 0.0)
    dstates = jnp.concatenate(
        [exact_dot(dinner, parts["out_state"], ROWS), exact_dot(dinner, parts["in_state"])],
        axis=1,
    )
    sig, pre = parts["states_sig"], parts["states_pre"]
    dpre = dstates * sig * (1.0 + pre * (1.0 - sig))
    back, rows = conv_backward(dpre, parts["states"], parts["bc"], pos)
    dp_ref[:, base : base + 2 * STATE] = back.astype(low)
    dbc_ref[...] = jnp.concatenate(rows, axis=0)

    pairs, keys, values = attention_parts(p_ref, cos_ref, sin_ref)
    cosine, sine = cos_ref[...], sin_ref[...]
    dkeys = [jnp.zeros((length, LANES), jnp.float32) for _ in range(2)]
    dvalues = [jnp.zeros((length, LANES), jnp.float32) for _ in range(2)]
    for i, query in enumerate(pairs):
        a = WIDTH + i * LANES
        datt = grad_all[:, a : a + LANES].astype(jnp.bfloat16)
        dquery = jnp.zeros((length, LANES), jnp.float32)
        for which in range(2):
            probs = attention_probs(query, keys[which], parts["same"])
            dprobs = low_dot(datt, values[which], COLS)
            dscores = probs * (dprobs - jnp.sum(probs * dprobs, axis=1, keepdims=True))
            dscores = dscores.astype(jnp.bfloat16)
            dquery = dquery + low_dot(dscores, keys[which])
            dkeys[which] = dkeys[which] + low_dot(dscores, query, ROWS)
            dvalues[which] = dvalues[which] + low_dot(probs, datt, ROWS)
        a = 2 * WIDTH + i * LANES
        dquery = turn_back(dquery * HEAD_A ** (-0.5), cosine, sine)
        dp_ref[:, a : a + LANES] = dquery.astype(low)
    dkey = half_lanes(dkeys[0], 0) + pltpu.roll(half_lanes(dkeys[1], 1), HEAD_A, 1)
    dvalue = pltpu.roll(half_lanes(dvalues[0], 0), HEAD_A, 1) + half_lanes(dvalues[1], 1)
    a = 2 * WIDTH + QCOLS
    dboth = half_lanes(turn_back(dkey, cosine, sine), 0) + dvalue
    dp_ref[:, a : a + LANES] = dboth.astype(low)
    half = dp_ref.shape[1] // 2
    split_columns(dp_ref[:, :half], dp_ref[:, half:], tidx_ref[1], keep_ref, give_ref)


def local_call(kernel, outs, name, scalars=0, after=0):
    space = pl.BlockSpec(memory_space=pltpu.VMEM)
    scalar = pl.BlockSpec(memory_space=pltpu.SMEM)
    return lambda *args: pl.pallas_call(
        kernel,
        out_shape=[jax.ShapeDtypeStruct(shape, dtype) for shape, dtype in outs],
        in_specs=[scalar] * scalars
        + [space] * (len(args) - scalars - after)
        + [pl.BlockSpec(memory_space=pl.ANY)] * after,
        out_specs=[space] * len(outs),
        compiler_params=pltpu.CompilerParams(vmem_limit_bytes=56 * 2**20),
        name=name,
    )(*args)


def mixer_consts(head_params, conv_shared, lens, where, length):
    _, pos = doc_index(lens, length)
    half = HEAD_A // 2
    freq = THETA ** (-jnp.arange(half, dtype=jnp.float32) * 2.0 / HEAD_A)
    angle = pos.astype(jnp.float32)[:, None] * freq[None, :]
    cosine, sine = jnp.cos(angle), jnp.sin(angle)
    heads = jnp.pad(
        head_params, ((0, 16 - HEADS), (0, 3 * LANES - head_params.shape[1]))
    )
    scalars = (where, lens)
    return scalars, (
        heads,
        conv_shared,
        jnp.concatenate([cosine] * 4, axis=1),
        jnp.concatenate([-sine, sine, -sine, sine], axis=1),
    )


def mixer_forward(projected, consts, weight):
    length = projected.shape[0]
    width = WIDTH + QCOLS
    outs = [
        ((length, width), jnp.bfloat16),
        ((length, WIDTH), jnp.float32),
        ((length // 2, weight.shape[0]), jnp.float32),
        ((length // 2, weight.shape[0]), jnp.bfloat16),
        ((length, width // 2), jnp.bfloat16),
        ((length, width // 2), jnp.bfloat16),
    ]
    scalars, arrays = consts
    return local_call(forward_kernel, outs, "mixer_forward", 2)(
        *scalars, projected, *arrays, weight
    )


def mixer_backward(projected, consts, outputs, grad, weight):
    length, width = projected.shape
    outs = [
        ((length, width), jnp.bfloat16),
        ((16, 3 * LANES), jnp.float32),
        ((CONV + 1, 2 * STATE), jnp.float32),
        ((length, width // 2), jnp.bfloat16),
        ((length, width // 2), jnp.bfloat16),
    ]
    scalars, arrays = consts
    grad_proj, heads, bc, keep, give = local_call(backward_kernel, outs, "mixer_backward", 2)(
        *scalars, projected, *arrays, outputs, grad, weight
    )
    return grad_proj, heads[:HEADS, : BIAS_COL + 1], bc, keep, give


def feed_kernel(
    where_ref, x_ref, grad_ref, w_ref,
    act_ref, dgu_ref, mine_ref, theirs_ref, keep_ref, give_ref, act_keep_ref, act_give_ref,
):
    units = act_ref.shape[1]
    tidx, core = where_ref[0], where_ref[1]
    gate_up = dot(x_ref[...], w_ref[:, : 2 * units])
    gate, upper = gate_up[:, :units], gate_up[:, units:]
    sig = jax.nn.sigmoid(gate)
    raised = gate * sig
    act = (raised * upper).astype(act_ref.dtype)
    act_ref[...] = act
    split_columns(act[:, : units // 2], act[:, units // 2 :], core, act_keep_ref, act_give_ref)
    grad = dot(grad_ref[...], w_ref[:, 2 * units : 3 * units])
    dgate = (grad * upper * sig * (1.0 + gate * (1.0 - sig))).astype(dgu_ref.dtype)
    dupper = (grad * raised).astype(dgu_ref.dtype)
    dgu_ref[:, :units] = dgate
    dgu_ref[:, units:] = dupper
    split_columns(dgate, dupper, core, keep_ref, give_ref)
    split_rows(dot_t(dgu_ref[...], w_ref[:, : 2 * units]), tidx, mine_ref, theirs_ref)


def feed_forward_back(where, values, grad, weight, units):
    length, width = values.shape
    low = jnp.bfloat16
    outs = [
        ((length, units), low),
        ((length, 2 * units), low),
        ((length // 2, width), jnp.float32),
        ((length // 2, width), low),
        ((length, units), low),
        ((length, units), low),
        ((length, units // 2), low),
        ((length, units // 2), low),
    ]
    return local_call(feed_kernel, outs, "feed_forward_back", 1)(where, values, grad, weight)


def middle_back(mine, taken, middle, gain, out_grad, *after):
    low = jnp.bfloat16

    def kernel(mine_ref, taken_ref, middle_ref, gain_ref, out_ref, *refs):
        grad_ref, low_ref, gain_grad_ref = refs[len(after) :]
        grad = mine_ref[...] + taken_ref[...].astype(jnp.float32)
        values = middle_ref[...]
        total = out_ref[...] + norm_back(values, gain_ref[...], grad)
        grad_ref[...] = total
        low_ref[...] = total.astype(low)
        gain_grad_ref[...] = jnp.sum(grad * values * norm_scale(values), axis=0, keepdims=True)

    shape = middle.shape
    outs = [(shape, jnp.float32), (shape, low), ((1, shape[1]), jnp.float32)]
    return local_call(kernel, outs, "middle_back", 0, len(after))(
        mine, taken, middle, gain[None, :], out_grad, *after
    )


def first_back(where, grad_proj, weight, resid, *after):
    def kernel(where_ref, dp_ref, w_ref, resid_ref, *refs):
        mine_ref, theirs_ref, gain_grad_ref = refs[len(after) :]
        grad = dot_t(dp_ref[...], w_ref[:, : dp_ref.shape[1]])
        values = resid_ref[...]
        gain_grad_ref[...] = jnp.sum(grad * values * norm_scale(values), axis=0, keepdims=True)
        split_rows(grad, where_ref[0], mine_ref, theirs_ref)

    rows, width = resid.shape
    outs = [
        ((rows // 2, width), jnp.float32),
        ((rows // 2, width), jnp.bfloat16),
        ((1, width), jnp.float32),
    ]
    return local_call(kernel, outs, "first_back", 1, len(after))(
        where, grad_proj, weight, resid, *after
    )


def feed_out(where, act, weight, *after):
    def kernel(where_ref, act_ref, w_ref, *refs):
        units = act_ref.shape[1]
        out = dot_t(act_ref[...], w_ref[:, 2 * units :])
        split_rows(out, where_ref[0], *refs[len(after) :])

    rows, width = act.shape[0] // 2, weight.shape[0]
    outs = [((rows, width), jnp.float32), ((rows, width), jnp.bfloat16)]
    return local_call(kernel, outs, "feed_out", 1, len(after))(where, act, weight, *after)


def weight_grads(sides, dtype):
    width = sum(side[1].shape[1] for side in sides)
    model = sides[0][0].shape[1]
    block = 256

    def kernel(*refs):
        out_ref, a = refs[-1], 0
        for i in range(len(sides)):
            x, y, other_x, other_y = refs[4 * i : 4 * i + 4]
            b = a + y.shape[1]
            for r in range(0, model, block):
                part = cross(x[:, r : r + block], y[...])
                part = part + cross(other_x[:, r : r + block], other_y[...])
                out_ref[r : r + block, a:b] = part.astype(out_ref.dtype)
            a = b

    flat = [value for side in sides for value in side]
    return local_call(kernel, [((model, width), dtype)], "weight_grads")(*flat)[0]


def cross(left, right):
    return lax.dot_general(
        left, right, (((0,), (0,)), ((), ())), preferred_element_type=jnp.float32
    )


def dot(left, right):
    return jnp.dot(left, right, preferred_element_type=jnp.float32)


def dot_t(left, right):
    return lax.dot_general(
        left, right, (((1,), (1,)), ((), ())), preferred_element_type=jnp.float32
    )


def adamw(weight, first, second, grad, rate, decay):
    first = 0.9 * first + 0.1 * grad
    second = 0.95 * second + 0.05 * grad * grad
    fixed_one = first / (1.0 - 0.9**STEP)
    fixed_two = second / (1.0 - 0.95**STEP)
    weight = weight - rate * (fixed_one / (jnp.sqrt(fixed_two) + 1e-08) + decay * weight)
    return (first, second, weight)


def swap(values, axis, distance):
    count = lax.axis_size(axis)
    return lax.ppermute(values, axis, [(i, i ^ distance) for i in range(count)])


def pair_rows(own, other, tidx):
    return jnp.where(
        tidx == 0,
        jnp.concatenate([own, other], axis=0),
        jnp.concatenate([other, own], axis=0),
    )


def gather_rows(own, tidx):
    return pair_rows(own, swap(own, "tensor", 1), tidx)


RING_CHIPS = 8


def ring_chip(place):
    place = place % RING_CHIPS
    half = RING_CHIPS // 2
    if isinstance(place, int):
        return 2 * place if place < half else 2 * (RING_CHIPS - 1 - place) + 1
    return jnp.where(place < half, 2 * place, 2 * (RING_CHIPS - 1 - place) + 1)


def ring_place(chip):
    return jnp.where(chip % 2 == 0, chip // 2, RING_CHIPS - 1 - chip // 2)


def ring_step(values):
    pairs = []
    for p in range(RING_CHIPS):
        pairs.append((CORES * ring_chip(p), CORES * ring_chip(p + 1)))
        pairs.append((CORES * ring_chip(p + 1) + 1, CORES * ring_chip(p) + 1))
    return lax.ppermute(values, "dp", pairs)


def place_rows(pieces, blocks, values=None, columns=0):
    count = len(pieces)
    height, width = pieces[0].shape
    low = pieces[0].dtype
    extra = [] if values is None else [values]

    def kernel(block_ref, *refs):
        out_ref = refs[count + len(extra)]
        for i in range(count):
            start = pl.multiple_of(block_ref[i] * height, height)
            out_ref[pl.ds(start, height), :] = refs[i][...]
        if extra:
            refs[-1][...] = dot(refs[count][...], out_ref[:, :columns]).astype(low)

    outs = [((count * height, width), low)]
    if extra:
        outs.append(((values.shape[0], columns), low))
    return local_call(kernel, outs, "place_rows", 1)(blocks, *pieces, *extra)


def ring_gather(shard, place, core):
    way = 1 - 2 * core
    own = [shard]
    other = [swap(shard, "dp", 1)]
    for _ in range(1, RING_CHIPS):
        own.append(ring_step(own[-1]))
        other.append(swap(own[-1], "dp", 1))
    blocks = [CORES * ring_chip(place - way * k) + core for k in range(RING_CHIPS)]
    blocks += [CORES * ring_chip(place + way * k) + 1 - core for k in range(RING_CHIPS)]
    return own + other, jnp.stack(blocks).astype(jnp.int32), own


def ring_reduce(chains, place, core, rider, last):
    way = 1 - 2 * core
    sums = [None] * len(chains)
    riders = [rider]
    for step in range(1, RING_CHIPS + 1):
        chip = ring_chip(place - way * step)
        for i, chain in enumerate(chains):
            if step == RING_CHIPS and i == 0:
                sums[0], last = lax.optimization_barrier((sums[0], last))
            parts = []
            for grad, a, b in chain:
                rows = grad.shape[0] // RING_CHIPS
                parts.append(lax.dynamic_slice(grad, (chip * rows, a), (rows, b - a)))
            part = parts[0] if len(parts) == 1 else jnp.concatenate(parts, axis=1)
            if step > 1:
                part = part + sums[i].astype(jnp.float32)
            if step < RING_CHIPS:
                part = part.astype(jnp.bfloat16)
                if i == 1:
                    width = part.shape[1]
                    part = ring_step(jnp.concatenate([part, riders[-1]], axis=1))
                    riders.append(part[:, width:])
                    part = part[:, :width]
                else:
                    part = ring_step(part)
            sums[i] = part
        if step == 1:
            first = sums[0]
    stack = jnp.stack(riders)
    total = 0.0
    for p in range(RING_CHIPS):
        taken = lax.dynamic_index_in_dim(
            stack, (way * (place - p)) % RING_CHIPS, axis=0, keepdims=False
        )
        total = total + taken.astype(jnp.float32)
    return jnp.concatenate(sums, axis=1), total, first, last


def both_cores(model_side, keep, give):
    return model_side, keep, swap(model_side, "dp", 1), swap(give, "dp", 1)


def own_rows(summed, core, extra=None):
    rows = summed.shape[0] // CORES
    upper, lower = summed[:rows], summed[rows:]
    mine = jnp.where(core == 0, upper, lower)
    give = jnp.where(core == 0, lower, upper).astype(jnp.bfloat16)
    if extra is None:
        taken = swap(give, "dp", 1).astype(jnp.float32)
        return jnp.where(core == 0, mine, taken), jnp.where(core == 0, taken, mine)
    width = give.shape[1]
    extra = extra.astype(jnp.bfloat16)
    taken = swap(jnp.concatenate([give, extra], axis=1), "dp", 1)
    extra = extra.astype(jnp.float32) + taken[:, width:].astype(jnp.float32)
    taken = taken[:, :width].astype(jnp.float32)
    return jnp.where(core == 0, mine, taken), jnp.where(core == 0, taken, mine), extra


def join_halves(halves, a, b):
    return jnp.concatenate([halves[0][:, a:b], halves[1][:, a:b]], axis=1)


def sum_all(values, axis):
    distance = 1
    while distance < lax.axis_size(axis):
        values = values + swap(values, axis, distance)
        distance *= 2
    return values


def per_device(
    residual,
    out_grad,
    doc_lengths,
    mixer_weight,
    mixer_first,
    mixer_second,
    scan_weight,
    scan_first,
    scan_second,
    merge_weight,
    merge_first,
    merge_second,
    hidden_weight,
    hidden_first,
    hidden_second,
    down_weight,
    down_first,
    down_second,
    head_params,
    head_first,
    head_second,
    shared_params,
    shared_first,
    shared_second,
):
    low = jnp.bfloat16
    tidx = lax.axis_index("tensor")
    count = lax.axis_size("dp")
    chips = count // CORES
    core = lax.axis_index("dp") % CORES
    place = ring_place(lax.axis_index("dp") // CORES)
    group = residual.shape[0] * lax.axis_size("tensor")
    conv_shared = shared_params[2 * D :].reshape(CONV + 1, 2 * STATE)

    ring = chips == RING_CHIPS
    mix_cols = mixer_weight.shape[1]
    both_cols = mix_cols + scan_weight.shape[1]
    spare = jnp.zeros((mixer_weight.shape[0], -both_cols % 256), low)
    first_cols = both_cols + spare.shape[1]
    units = down_weight.shape[0]
    first_shard = jnp.concatenate(
        [mixer_weight.astype(low), scan_weight.astype(low), spare, merge_weight.astype(low).T],
        axis=1,
    )
    rest_shard = jnp.concatenate(
        [hidden_weight.astype(low), down_weight.astype(low).T], axis=1
    )
    where = jnp.stack([tidx, core]).astype(jnp.int32)
    consts = mixer_consts(head_params, conv_shared, doc_lengths[0], where, group)
    gain_one, gain_two = shared_params[:D], shared_params[D : 2 * D]
    resid_all = gather_rows(residual, tidx)
    first_all = scaled_norm(resid_all, gain_one).astype(low)
    grad_feed = gather_rows(out_grad.astype(low), tidx)
    if ring:
        pieces, blocks, own = ring_gather(first_shard, place, core)
        first_w, projected = place_rows(pieces, blocks, first_all, first_cols)
        rest_shard = lax.optimization_barrier((rest_shard, own[4]))[0]
    else:
        first_w = lax.all_gather(first_shard, "dp", axis=0, tiled=True)
        projected = dot(first_all, first_w[:, :first_cols]).astype(low)
    rest_w = lax.all_gather(rest_shard, "dp", axis=0, tiled=True)
    merge_w = first_w[:, first_cols:]
    joined_low, outputs, mine, theirs, joined_keep, joined_give = mixer_forward(
        projected, consts, first_w
    )
    middle = residual + mine + swap(theirs, "tensor", 1).astype(jnp.float32)
    second_all = gather_rows(scaled_norm(middle, gain_two).astype(low), tidx)
    activ_low, grad_gu, mine, theirs, gu_keep, gu_give, act_keep, act_give = feed_forward_back(
        where, second_all, grad_feed, rest_w, units
    )
    taken = swap(theirs, "tensor", 1)
    waits = []
    if ring:
        rest_grad = weight_grads(
            [
                both_cores(second_all, gu_keep, gu_give),
                both_cores(grad_feed, act_keep, act_give),
            ],
            low,
        )
        rest_sum = lax.psum_scatter(
            rest_grad,
            "dp",
            scatter_dimension=0,
            axis_index_groups=[[i * CORES + c for i in range(chips)] for c in range(CORES)],
            tiled=True,
        )
        waits = [rest_grad]
    grad_middle, grad_low, gain_two_grad = middle_back(
        mine, taken, middle, gain_two, out_grad, *waits
    )
    grad_mixed = gather_rows(grad_low, tidx)
    grad_proj, head_grad, conv_grad, proj_keep, proj_give = mixer_backward(
        projected, consts, outputs, grad_mixed, first_w
    )
    waits = []
    if ring:
        first_grad = weight_grads([both_cores(first_all, proj_keep, proj_give)], jnp.float32)
        waits = [first_grad]
    mine_first, theirs_first, gain_one_grad = first_back(
        where, grad_proj, first_w, resid_all, *waits
    )
    gain_one_grad, gain_two_grad = gain_one_grad.reshape(-1), gain_two_grad.reshape(-1)
    waits = []
    shared_part = jnp.concatenate([gain_one_grad, gain_two_grad, conv_grad.reshape(-1)])
    small = jnp.concatenate([shared_part, head_grad.reshape(-1)])
    if ring:
        rest_halves = own_rows(rest_sum.astype(jnp.float32), core)
        hidden_sum = join_halves(rest_halves, 0, units)
        down_sum = join_halves(rest_halves, units, rest_sum.shape[1]).T
        hidden_new = adamw(hidden_weight, hidden_first, hidden_second, hidden_sum, 0.02, 0.1)
        down_new = adamw(down_weight, down_first, down_second, down_sum, 0.02, 0.1)
        merge_grad = weight_grads([both_cores(grad_mixed, joined_keep, joined_give)], jnp.float32)
        a = first_cols // CORES
        cut = (a + merge_grad.shape[1]) // 2 // 128 * 128
        chains = [
            [(first_grad, 0, cut)],
            [(first_grad, cut, a), (merge_grad, 0, merge_grad.shape[1])],
        ]
        rows = D // RING_CHIPS
        rider = jnp.pad(small.astype(low), (0, rows * LANES - small.shape[0]))
        first_sum, small_sum, mark, (hidden_new, down_new) = ring_reduce(
            chains, place, core, rider.reshape(rows, LANES), (hidden_new, down_new)
        )
        waits = [mark]
        half = rows // CORES
        small_sum = jnp.concatenate([small_sum[:half], small_sum[half:]], axis=1)
        first_halves = own_rows(first_sum, core, small_sum)
        merge_sum = join_halves(first_halves, a, first_sum.shape[1]).T
        first_sum = join_halves(first_halves, 0, a)
    else:
        whole = jnp.concatenate(
            [
                cross(first_all, grad_proj),
                cross(second_all, grad_gu),
                cross(grad_feed, activ_low),
                cross(grad_mixed, joined_low),
            ],
            axis=1,
        ).astype(low)
        whole = lax.psum_scatter(whole, "dp", scatter_dimension=0, tiled=True)
        whole = whole.astype(jnp.float32)
        a = grad_proj.shape[1]
        first_sum = whole[:, :a]
        hidden_sum = whole[:, a : a + 2 * units]
        a = a + 2 * units
        down_sum = whole[:, a : a + units].T
        merge_sum = whole[:, a + units :].T
        hidden_new = adamw(hidden_weight, hidden_first, hidden_second, hidden_sum, 0.02, 0.1)
        down_new = adamw(down_weight, down_first, down_second, down_sum, 0.02, 0.1)
    mixer_sum, scan_sum = first_sum[:, :mix_cols], first_sum[:, mix_cols:both_cols]
    split = shared_part.shape[0]
    if ring:
        both = jnp.concatenate([scan_sum, first_halves[2]], axis=1)
        taken = swap(both, "tensor", 1)
        scan_sum = scan_sum + taken[:, : scan_sum.shape[1]]
        own_sum = jnp.concatenate([first_halves[2][:, :LANES], first_halves[2][:, LANES:]], axis=0)
        taken = taken[:, scan_sum.shape[1] :]
        taken = jnp.concatenate([taken[:, :LANES], taken[:, LANES:]], axis=0)
        shared_sum = (own_sum + taken).reshape(-1)[:split]
        head_sum = own_sum.reshape(-1)[split : small.shape[0]].reshape(head_grad.shape)
    else:
        scan_sum = scan_sum + swap(scan_sum, "tensor", 1)
        small = sum_all(small, "dp")
        shared_sum = sum_all(small[:split], "tensor")
        head_sum = small[split:].reshape(head_grad.shape)
    grad_first = mine_first + swap(theirs_first, "tensor", 1).astype(jnp.float32)
    input_grad = grad_middle + norm_back(residual, gain_one, grad_first)
    mine, theirs = feed_out(where, activ_low, rest_w, *waits)
    block_out = middle + mine + swap(theirs, "tensor", 1).astype(jnp.float32)

    mixer_new = adamw(mixer_weight, mixer_first, mixer_second, mixer_sum, 0.02, 0.1)
    scan_new = adamw(scan_weight, scan_first, scan_second, scan_sum, 0.02, 0.1)
    merge_new = adamw(merge_weight, merge_first, merge_second, merge_sum, 0.02, 0.1)
    head_new = adamw(head_params, head_first, head_second, head_sum, 0.2, 0.0)
    shared_new = adamw(shared_params, shared_first, shared_second, shared_sum, 0.2, 0.0)
    return (
        block_out,
        input_grad,
        *mixer_new,
        *scan_new,
        *merge_new,
        *hidden_new,
        *down_new,
        *head_new,
        *shared_new,
    )


def solution(mesh):
    return jax.shard_map(
        per_device,
        mesh=mesh,
        in_specs=(
            P(("dp", "tensor"), None),
            P(("dp", "tensor"), None),
            P("dp", None),
            P("dp", "tensor"),
            P("dp", "tensor"),
            P("dp", "tensor"),
            P("dp", None),
            P("dp", None),
            P("dp", None),
            P("tensor", "dp"),
            P("tensor", "dp"),
            P("tensor", "dp"),
            P("dp", "tensor"),
            P("dp", "tensor"),
            P("dp", "tensor"),
            P("tensor", "dp"),
            P("tensor", "dp"),
            P("tensor", "dp"),
            P("tensor", None),
            P("tensor", None),
            P("tensor", None),
            P(),
            P(),
            P(),
        ),
        out_specs=(
            P(("dp", "tensor"), None),
            P(("dp", "tensor"), None),
            P("dp", "tensor"),
            P("dp", "tensor"),
            P("dp", "tensor"),
            P("dp", None),
            P("dp", None),
            P("dp", None),
            P("tensor", "dp"),
            P("tensor", "dp"),
            P("tensor", "dp"),
            P("dp", "tensor"),
            P("dp", "tensor"),
            P("dp", "tensor"),
            P("tensor", "dp"),
            P("tensor", "dp"),
            P("tensor", "dp"),
            P("tensor", None),
            P("tensor", None),
            P("tensor", None),
            P(),
            P(),
            P(),
        ),
        check_vma=False,
    )
```

profile of v0, /device:TPU:0, one launch (start us, length us, event | category | flops | bytes accessed | tf_op | source)
XLA Modules:
  0.0 294.4 jit_solution(15677835499055077808)
XLA Ops:
  10.4 3.1 %collective-permute-start = (bf16[64,3328]{1,0:T(8,128)(2,1)S(1)}, bf16[64,3328]{1,0:T(8,128)(2,1)S(1)}, u32[]{:S(2)}, u32[]{:S(2)}) collective-permute-start(bf16[64,3328]{1,0:T(8,128)(2,1)S(1)} %concatenate.117.refs_0_), channel_id=1, source_target_pairs={{0,8},{10,2},{8,16},{18,10},{16,24},{26,18},{24,28},{30,26},{28,20... | collective-permute-start | bytes 1277960 | tf_op jit(solution)/shard_map/ppermute | solution.py:623
  13.5 6.0 %collective-permute-done.refs_1_ = bf16[64,3328]{1,0:T(8,128)(2,1)S(1)} collective-permute-done((bf16[64,3328]{1,0:T(8,128)(2,1)S(1)}, bf16[64,3328]{1,0:T(8,128)(2,1)S(1)}, u32[]{:S(2)}, u32[]{:S(2)}) %collective-permute-start) | collective-permute-done | bytes 426016 | tf_op jit(solution)/shard_map/ppermute | solution.py:623
  21.6 6.0 %collective-permute-done.1.refs_2_ = bf16[64,3328]{1,0:T(8,128)(2,1)S(1)} collective-permute-done((bf16[64,3328]{1,0:T(8,128)(2,1)S(1)}, bf16[64,3328]{1,0:T(8,128)(2,1)S(1)}, u32[]{:S(2)}, u32[]{:S(2)}) %collective-permute-start.1) | collective-permute-done | bytes 426016 | tf_op jit(solution)/shard_map/ppermute | solution.py:623
  29.7 6.0 %collective-permute-done.2.refs_3_ = bf16[64,3328]{1,0:T(8,128)(2,1)S(1)} collective-permute-done((bf16[64,3328]{1,0:T(8,128)(2,1)S(1)}, bf16[64,3328]{1,0:T(8,128)(2,1)S(1)}, u32[]{:S(2)}, u32[]{:S(2)}) %collective-permute-start.2) | collective-permute-done | bytes 426016 | tf_op jit(solution)/shard_map/ppermute | solution.py:623
  40.7 3.3 %collective-permute-done.3.refs_4_ = bf16[64,3328]{1,0:T(8,128)(2,1)} collective-permute-done((bf16[64,3328]{1,0:T(8,128)(2,1)S(1)}, bf16[64,3328]{1,0:T(8,128)(2,1)}, u32[]{:S(2)}, u32[]{:S(2)}) %collective-permute-start.3) | collective-permute-done | bytes 426016 | tf_op jit(solution)/shard_map/ppermute | solution.py:623
  49.3 3.2 %collective-permute-done.4.refs_5_ = bf16[64,3328]{1,0:T(8,128)(2,1)} collective-permute-done((bf16[64,3328]{1,0:T(8,128)(2,1)}, bf16[64,3328]{1,0:T(8,128)(2,1)}, u32[]{:S(2)}, u32[]{:S(2)}) %collective-permute-start.4) | collective-permute-done | bytes 426016 | tf_op jit(solution)/shard_map/ppermute | solution.py:623
  58.9 10.6 %collective-permute-done.5.refs_6_ = bf16[64,3328]{1,0:T(8,128)(2,1)} collective-permute-done((bf16[64,3328]{1,0:T(8,128)(2,1)}, bf16[64,3328]{1,0:T(8,128)(2,1)}, u32[]{:S(2)}, u32[]{:S(2)}) %collective-permute-start.5) | collective-permute-done | bytes 426016 | tf_op jit(solution)/shard_map/ppermute | solution.py:623
  69.5 4.1 %collective-permute-start.6 = (bf16[64,3328]{1,0:T(8,128)(2,1)}, bf16[64,3328]{1,0:T(8,128)(2,1)S(1)}, u32[]{:S(2)}, u32[]{:S(2)}) collective-permute-start(bf16[64,3328]{1,0:T(8,128)(2,1)} %collective-permute-done.5.refs_6_), channel_id=1, source_target_pairs={{0,8},{10,2},{8,16},{18,10},{16,24},{26,18},{24,28},{30,26},{28,20... | collective-permute-start | bytes 1277960 | tf_op jit(solution)/shard_map/ppermute | solution.py:623
  75.6 5.8 %collective-permute-done.6.refs_7_ = bf16[64,3328]{1,0:T(8,128)(2,1)S(1)} collective-permute-done((bf16[64,3328]{1,0:T(8,128)(2,1)}, bf16[64,3328]{1,0:T(8,128)(2,1)S(1)}, u32[]{:S(2)}, u32[]{:S(2)}) %collective-permute-start.6) | collective-permute-done | bytes 426016 | tf_op jit(solution)/shard_map/ppermute | solution.py:623
  84.3 6.8 %place_rows.1 = (bf16[1024,3328]{1,0:T(8,128)(2,1)}, bf16[256,2304]{1,0:T(8,128)(2,1)}) custom-call(s32[16]{0:T(128)} %stack.103.block_ref, bf16[64,3328]{1,0:T(8,128)(2,1)} %copy-done.12, bf16[64,3328]{1,0:T(8,128)(2,1)} %copy-done.31, bf16[64,3328]{1,0:T(8,128)(2,1)} %copy-done.32, bf16[64,3328]{1,0:T(8,128)(2,1)} %copy-done.33, ...), custom_call_target="tpu_custom_call" | custom-call | tf_op jit(solution)/shard_map/place_rows/pallas_call | solution.py:391
  91.1 9.3 %mixer_forward.1 = (bf16[256,1024]{1,0:T(8,128)(2,1)}, f32[256,768]{1,0:T(8,128)}, f32[128,1024]{1,0:T(8,128)}, bf16[128,1024]{1,0:T(8,128)(2,1)}, bf16[256,512]{1,0:T(8,128)(2,1)}, /*index=5*/bf16[256,512]{1,0:T(8,128)(2,1)}) custom-call(s32[2]{0:T(128)} %pad_add_fusion.tidx_ref.where_ref, s32[4]{0:T(128)} %bitcast.75, ...), custom_call_target="tpu_custom_call" | custom-call | tf_op jit(solution)/shard_map/mixer_forward/pallas_call | solution.py:391
  102.6 7.2 %collective-permute-done.16 = bf16[128,1024]{1,0:T(8,128)(2,1)S(1)} collective-permute-done((bf16[128,1024]{1,0:T(8,128)(2,1)}, bf16[128,1024]{1,0:T(8,128)(2,1)S(1)}, u32[]{:S(2)}, u32[]{:S(2)}) %collective-permute-start.16) | collective-permute-done | bytes 262176 | tf_op jit(solution)/shard_map/ppermute | solution.py:588
  112.7 2.7 collective-permute-done.18
  115.6 5.0 %collective-permute-done.17 = bf16[128,1024]{1,0:T(8,128)(2,1)S(1)} collective-permute-done((bf16[128,1024]{1,0:T(8,128)(2,1)S(1)}, bf16[128,1024]{1,0:T(8,128)(2,1)S(1)}, u32[]{:S(2)}, u32[]{:S(2)}) %collective-permute-start.17) | collective-permute-done | bytes 262176 | tf_op jit(solution)/shard_map/ppermute | solution.py:588
  121.6 7.5 %feed_forward_back.1 = (bf16[256,1024]{1,0:T(8,128)(2,1)}, bf16[256,2048]{1,0:T(8,128)(2,1)}, f32[128,1024]{1,0:T(8,128)}, bf16[128,1024]{1,0:T(8,128)(2,1)}, bf...) custom-call(s32[2]{0:T(128)} %pad_add_fusion.tidx_ref.where_ref, ...), custom_call_target="tpu_custom_call" | custom-call | tf_op jit(solution)/shard_map/feed_forward_back/pallas_call | solution.py:391
  132.6 5.7 %weight_grads.3.refs_0_ = bf16[1024,1536]{1,0:T(8,128)(2,1)} custom-call(bf16[256,1024]{1,0:T(8,128)(2,1)} %copy-done.7, bf16[256,1024]{1,0:T(8,128)(2,1)} %get-tuple-element.67.refs_1_, bf16[256,1024]{1,0:T(8,128)(2,1)} %copy-done.27, bf16[256,1024]{1,0:T(8,128)(2,1)} %copy-done.28, bf16[256,1024]{1,0:T(8,128)(2,1)} %copy-done.6, ...), custom_call_target="tpu_custom_call" | custom-call | tf_op jit(solution)/shard_map/weight_grads/pallas_call | solution.py:391
  143.1 7.1 %collective-permute-done.24 = bf16[128,1024]{1,0:T(8,128)(2,1)S(1)} collective-permute-done((bf16[128,1024]{1,0:T(8,128)(2,1)}, bf16[128,1024]{1,0:T(8,128)(2,1)S(1)}, u32[]{:S(2)}, u32[]{:S(2)}) %collective-permute-start.24) | collective-permute-done | bytes 262176 | tf_op jit(solution)/shard_map/ppermute | solution.py:588
  152.2 15.4 %mixer_backward.1 = (bf16[256,2304]{1,0:T(8,128)(2,1)}, f32[16,384]{1,0:T(8,128)}, f32[5,256]{1,0:T(8,128)}, bf16[256,1152]{1,0:T(8,128)(2,1)}, bf16[256,1152]{1,0:T(8,128)(2,1)}) custom-call(s32[2]{0:T(128)} %pad_add_fusion.tidx_ref.where_ref, s32[4]{0:T(128)} %bitcast.76, bf16[256,2304]{1,0:T(8,128)(2,1)} %get-tuple-element.58.p_ref, ...), custom_call_target="tpu_custom_call" | custom-call | tf_op jit(solution)/shard_map/mixer_backward/pallas_call | solution.py:391
  171.4 3.7 %weight_grads.5 = f32[1024,512]{1,0:T(8,128)} custom-call(bf16[256,1024]{1,0:T(8,128)(2,1)} %copy-done.4, bf16[256,512]{1,0:T(8,128)(2,1)} %get-tuple-element.81.refs_1_, bf16[256,1024]{1,0:T(8,128)(2,1)} %copy-done.24, bf16[256,512]{1,0:T(8,128)(2,1)} %copy-done.44), custom_call_target="tpu_custom_call" | custom-call | tf_op jit(solution)/shard_map/weight_grads/pallas_call | solution.py:391
  178.6 5.3 %weight_grads.4.refs_0_ = f32[1024,1152]{1,0:T(8,128)} custom-call(bf16[256,1024]{1,0:T(8,128)(2,1)} %multiply_convert_fusion.refs_16_.refs_0_, bf16[256,1152]{1,0:T(8,128)(2,1)} %get-tuple-element.72.refs_1_, bf16[256,1024]{1,0:T(8,128)(2,1)} %collective-permute-done.25.refs_2_, bf16[256,1152]{1,0:T(8,128)(2,1)} %copy-done.21), custom_call_target="tpu_custom_call" | custom-call | tf_op jit(solution)/shard_map/weight_grads/pallas_call | solution.py:391
  189.0 3.9 %collective-permute-start.27 = (bf16[128,768]{1,0:T(8,128)(2,1)}, bf16[128,768]{1,0:T(8,128)(2,1)S(1)}, u32[]{:S(2)}, u32[]{:S(2)}) collective-permute-start(bf16[128,768]{1,0:T(8,128)(2,1)} %dynamic-slice_convert_fusion), channel_id=1, source_target_pairs={{0,8},{10,2},{8,16},{18,10},{16,24},{26,18},{24,28},{30,26},{28,20... | collective-permute-start | bytes 589832 | tf_op jit(solution)/shard_map/ppermute | solution.py:623
  192.9 6.2 %first_back.1 = (f32[128,1024]{1,0:T(8,128)}, bf16[128,1024]{1,0:T(8,128)(2,1)}, f32[1,1024]{1,0:T(1,128)}) custom-call(s32[2]{0:T(128)} %pad_add_fusion.tidx_ref.where_ref, bf16[256,2304]{1,0:T(8,128)(2,1)} %get-tuple-element.77.dp_ref, bf16[1024,3328]{1,0:T(8,128)(2,1)} %get-tuple-element.59.w_ref, f32[256,1024]{1,0:T(8,128)} %copy-done, ...), custom_call_target="tpu_custom_call" | custom-call | tf_op jit(solution)/shard_map/first_back/pallas_call | solution.py:391
  200.6 2.7 collective-permute-start.39
  206.3 4.7 %feed_out.1 = (f32[128,1024]{1,0:T(8,128)}, bf16[128,1024]{1,0:T(8,128)(2,1)}) custom-call(s32[2]{0:T(128)} %pad_add_fusion.tidx_ref.where_ref, bf16[256,1024]{1,0:T(8,128)(2,1)} %get-tuple-element.63.act_ref, bf16[1024,3072]{1,0:T(8,128)(2,1)} %all-gather.2.cloned.1.call-done.w_ref, bf16[128,768]{1,0:T(8,128)(2,1)} %copy-done.15), custom_call_target="tpu_custom_call" | custom-call | tf_op jit(solution)/shard_map/feed_out/pallas_call | solution.py:391
  214.5 3.3 %collective-permute-start.40 = (bf16[128,1024]{1,0:T(8,128)(2,1)S(1)}, bf16[128,1024]{1,0:T(8,128)(2,1)S(1)}, u32[]{:S(2)}, u32[]{:S(2)}) collective-permute-start(bf16[128,1024]{1,0:T(8,128)(2,1)S(1)} %pad_maximum_fusion.5), channel_id=1, source_target_pairs={{0,8},{10,2},{8,16},{18,10},{16,24},{26,18},{24,28},{30,26},{28,20... | collective-permute-start | bytes 786440 | tf_op jit(solution)/shard_map/ppermute | solution.py:623
  221.7 3.3 %collective-permute-done.40 = bf16[128,1024]{1,0:T(8,128)(2,1)S(1)} collective-permute-done((bf16[128,1024]{1,0:T(8,128)(2,1)S(1)}, bf16[128,1024]{1,0:T(8,128)(2,1)S(1)}, u32[]{:S(2)}, u32[]{:S(2)}) %collective-permute-start.40) | collective-permute-done | bytes 262176 | tf_op jit(solution)/shard_map/ppermute | solution.py:623
  227.5 4.1 %collective-permute-done.41 = bf16[128,1024]{1,0:T(8,128)(2,1)S(1)} collective-permute-done((bf16[128,1024]{1,0:T(8,128)(2,1)S(1)}, bf16[128,1024]{1,0:T(8,128)(2,1)S(1)}, u32[]{:S(2)}, u32[]{:S(2)}) %collective-permute-start.41) | collective-permute-done | bytes 262176 | tf_op jit(solution)/shard_map/ppermute | solution.py:623
  233.7 4.3 %collective-permute-done.42 = bf16[128,1024]{1,0:T(8,128)(2,1)S(1)} collective-permute-done((bf16[128,1024]{1,0:T(8,128)(2,1)S(1)}, bf16[128,1024]{1,0:T(8,128)(2,1)S(1)}, u32[]{:S(2)}, u32[]{:S(2)}) %collective-permute-start.42) | collective-permute-done | bytes 262176 | tf_op jit(solution)/shard_map/ppermute | solution.py:623
  238.3 5.7 %collective-permute-done.33 = bf16[128,768]{1,0:T(8,128)(2,1)S(1)} collective-permute-done((bf16[128,768]{1,0:T(8,128)(2,1)S(1)}, bf16[128,768]{1,0:T(8,128)(2,1)S(1)}, u32[]{:S(2)}, u32[]{:S(2)}) %collective-permute-start.33) | collective-permute-done | bytes 196640 | tf_op jit(solution)/shard_map/ppermute | solution.py:623
  244.1 5.3 %collective-permute-done.43 = bf16[128,1024]{1,0:T(8,128)(2,1)S(1)} collective-permute-done((bf16[128,1024]{1,0:T(8,128)(2,1)S(1)}, bf16[128,1024]{1,0:T(8,128)(2,1)S(1)}, u32[]{:S(2)}, u32[]{:S(2)}) %collective-permute-start.43) | collective-permute-done | bytes 262176 | tf_op jit(solution)/shard_map/ppermute | solution.py:623
  252.0 3.2 %collective-permute-done.34 = bf16[128,768]{1,0:T(8,128)(2,1)S(1)} collective-permute-done((bf16[128,768]{1,0:T(8,128)(2,1)S(1)}, bf16[128,768]{1,0:T(8,128)(2,1)S(1)}, u32[]{:S(2)}, u32[]{:S(2)}) %collective-permute-start.34) | collective-permute-done | bytes 196640 | tf_op jit(solution)/shard_map/ppermute | solution.py:623
  260.8 4.2 %collective-permute-done.45 = bf16[128,1024]{1,0:T(8,128)(2,1)S(1)} collective-permute-done((bf16[128,1024]{1,0:T(8,128)(2,1)S(1)}, bf16[128,1024]{1,0:T(8,128)(2,1)S(1)}, u32[]{:S(2)}, u32[]{:S(2)}) %collective-permute-start.45) | collective-permute-done | bytes 262176 | tf_op jit(solution)/shard_map/ppermute | solution.py:623
  (310 shorter events, 103.7 us)
Async XLA Ops:
  7.2 113.7 %all-gather.2.cloned.1.call-start = ((), (), s32[]{:S(2)}) async-start(), calls=%async_computation.1 | async-start | bytes 6684672 | tf_op jit(solution)/shard_map/all_gather | solution.py:789
  10.4 9.1 %collective-permute-start = (bf16[64,3328]{1,0:T(8,128)(2,1)S(1)}, bf16[64,3328]{1,0:T(8,128)(2,1)S(1)}, u32[]{:S(2)}, u32[]{:S(2)}) collective-permute-start(bf16[64,3328]{1,0:T(8,128)(2,1)S(1)} %concatenate.117.refs_0_), channel_id=1, source_target_pairs={{0,8},{10,2},{8,16},{18,10},{16,24},{26,18},{24,28},{30,26},{28,20... | collective-permute-start | bytes 1277960 | tf_op jit(solution)/shard_map/ppermute | solution.py:623
  19.5 8.1 %collective-permute-start.1 = (bf16[64,3328]{1,0:T(8,128)(2,1)S(1)}, bf16[64,3328]{1,0:T(8,128)(2,1)S(1)}, u32[]{:S(2)}, u32[]{:S(2)}) collective-permute-start(bf16[64,3328]{1,0:T(8,128)(2,1)S(1)} %collective-permute-done.refs_1_), channel_id=1, source_target_pairs={{0,8},{10,2},{8,16},{18,10},{16,24},{26,18},{24,28},{30,26},{28,20... | collective-permute-start | bytes 1277960 | tf_op jit(solution)/shard_map/ppermute | solution.py:623
  35.7 8.2 %collective-permute-start.3 = (bf16[64,3328]{1,0:T(8,128)(2,1)S(1)}, bf16[64,3328]{1,0:T(8,128)(2,1)}, u32[]{:S(2)}, u32[]{:S(2)}) collective-permute-start(bf16[64,3328]{1,0:T(8,128)(2,1)S(1)} %collective-permute-done.2.refs_3_), channel_id=1, source_target_pairs={{0,8},{10,2},{8,16},{18,10},{16,24},{26,18},{24,28},{30,26},{28,20... | collective-permute-start | bytes 1277960 | tf_op jit(solution)/shard_map/ppermute | solution.py:623
  44.0 221.2 %reduce-scatter.2.cloned.1.call-start = ((), (), s32[]{:S(2)}) async-start(), calls=%async_computation.2 | async-start | bytes 3538944 | tf_op jit(solution)/shard_map/reduce_scatter | solution.py:809
  44.1 8.5 %collective-permute-start.4 = (bf16[64,3328]{1,0:T(8,128)(2,1)}, bf16[64,3328]{1,0:T(8,128)(2,1)}, u32[]{:S(2)}, u32[]{:S(2)}) collective-permute-start(bf16[64,3328]{1,0:T(8,128)(2,1)} %collective-permute-done.3.refs_4_), channel_id=1, source_target_pairs={{0,8},{10,2},{8,16},{18,10},{16,24},{26,18},{24,28},{30,26},{28,20... | collective-permute-start | bytes 1277960 | tf_op jit(solution)/shard_map/ppermute | solution.py:623
  46.2 28.4 %collective-permute-start.7 = (bf16[64,3328]{1,0:T(8,128)(2,1)S(1)}, bf16[64,3328]{1,0:T(8,128)(2,1)}, u32[]{:S(2)}, u32[]{:S(2)}) collective-permute-start(bf16[64,3328]{1,0:T(8,128)(2,1)S(1)} %concatenate.117.refs_0_), channel_id=1, source_target_pairs={{0,2},{2,0},{4,6},{6,4},{8,10},{10,8},{12,14},{14,12},{16,18},{18,... | collective-permute-start | bytes 1277960 | tf_op jit(solution)/shard_map/ppermute | solution.py:588
  46.2 28.0 %collective-permute-start.15 = (f32[128,1024]{1,0:T(8,128)}, f32[128,1024]{1,0:T(8,128)S(1)}, u32[]{:S(2)}, u32[]{:S(2)}) collective-permute-start(f32[128,1024]{1,0:T(8,128)} %param.24), channel_id=1, source_target_pairs={{0,1},{1,0},{2,3},{3,2},{4,5},{5,4},{6,7},{7,6},{8,9},{9,8},{10,11... | collective-permute-start | bytes 1572872 | tf_op jit(solution)/shard_map/ppermute | solution.py:588
  52.5 17.0 %collective-permute-start.5 = (bf16[64,3328]{1,0:T(8,128)(2,1)}, bf16[64,3328]{1,0:T(8,128)(2,1)}, u32[]{:S(2)}, u32[]{:S(2)}) collective-permute-start(bf16[64,3328]{1,0:T(8,128)(2,1)} %collective-permute-done.4.refs_5_), channel_id=1, source_target_pairs={{0,8},{10,2},{8,16},{18,10},{16,24},{26,18},{24,28},{30,26},{28,20... | collective-permute-start | bytes 1277960 | tf_op jit(solution)/shard_map/ppermute | solution.py:623
  58.4 16.6 %collective-permute-start.8 = (bf16[64,3328]{1,0:T(8,128)(2,1)S(1)}, bf16[64,3328]{1,0:T(8,128)(2,1)S(1)}, u32[]{:S(2)}, u32[]{:S(2)}) collective-permute-start(bf16[64,3328]{1,0:T(8,128)(2,1)S(1)} %collective-permute-done.refs_1_), channel_id=1, source_target_pairs={{0,2},{2,0},{4,6},{6,4},{8,10},{10,8},{12,14},{14,12},{16,18},{18,... | collective-permute-start | bytes 1277960 | tf_op jit(solution)/shard_map/ppermute | solution.py:588
  58.4 16.7 %collective-permute-start.9 = (bf16[64,3328]{1,0:T(8,128)(2,1)S(1)}, bf16[64,3328]{1,0:T(8,128)(2,1)S(1)}, u32[]{:S(2)}, u32[]{:S(2)}) collective-permute-start(bf16[64,3328]{1,0:T(8,128)(2,1)S(1)} %collective-permute-done.1.refs_2_), channel_id=1, source_target_pairs={{0,2},{2,0},{4,6},{6,4},{8,10},{10,8},{12,14},{14,12},{16,18},{18,... | collective-permute-start | bytes 1277960 | tf_op jit(solution)/shard_map/ppermute | solution.py:588
  69.5 11.8 %collective-permute-start.6 = (bf16[64,3328]{1,0:T(8,128)(2,1)}, bf16[64,3328]{1,0:T(8,128)(2,1)S(1)}, u32[]{:S(2)}, u32[]{:S(2)}) collective-permute-start(bf16[64,3328]{1,0:T(8,128)(2,1)} %collective-permute-done.5.refs_6_), channel_id=1, source_target_pairs={{0,8},{10,2},{8,16},{18,10},{16,24},{26,18},{24,28},{30,26},{28,20... | collective-permute-start | bytes 1277960 | tf_op jit(solution)/shard_map/ppermute | solution.py:623
  100.4 9.4 %collective-permute-start.16 = (bf16[128,1024]{1,0:T(8,128)(2,1)}, bf16[128,1024]{1,0:T(8,128)(2,1)S(1)}, u32[]{:S(2)}, u32[]{:S(2)}) collective-permute-start(bf16[128,1024]{1,0:T(8,128)(2,1)} %get-tuple-element.61), channel_id=1, source_target_pairs={{0,1},{1,0},{2,3},{3,2},{4,5},{5,4},{6,7},{7,6},{8,9},{9,8},{10,11... | collective-permute-start | bytes 786440 | tf_op jit(solution)/shard_map/ppermute | solution.py:588
  102.0 13.4 %collective-permute-start.18 = (bf16[128,1024]{1,0:T(8,128)(2,1)S(1)}, bf16[128,1024]{1,0:T(8,128)(2,1)S(1)}, u32[]{:S(2)}, u32[]{:S(2)}) collective-permute-start(bf16[128,1024]{1,0:T(8,128)(2,1)S(1)} %convert_element_type.196), channel_id=1, source_target_pairs={{0,1},{1,0},{2,3},{3,2},{4,5},{5,4},{6,7},{7,6},{8,9},{9,8},{10,11... | collective-permute-start | bytes 786440 | tf_op jit(solution)/shard_map/ppermute | solution.py:588
  111.1 9.5 %collective-permute-start.17 = (bf16[128,1024]{1,0:T(8,128)(2,1)S(1)}, bf16[128,1024]{1,0:T(8,128)(2,1)S(1)}, u32[]{:S(2)}, u32[]{:S(2)}) collective-permute-start(bf16[128,1024]{1,0:T(8,128)(2,1)S(1)} %multiply_convert_fusion.1), channel_id=1, source_target_pairs={{0,1},{1,0},{2,3},{3,2},{4,5},{5,4},{6,7},{7,6},{8,9},{9,8},{10,11... | collective-permute-start | bytes 786440 | tf_op jit(solution)/shard_map/ppermute | solution.py:588
  115.6 15.6 %collective-permute-start.22 = (bf16[256,1024]{1,0:T(8,128)(2,1)S(1)}, bf16[256,1024]{1,0:T(8,128)(2,1)S(1)}, u32[]{:S(2)}, u32[]{:S(2)}) collective-permute-start(bf16[256,1024]{1,0:T(8,128)(2,1)S(1)} %maximum_select_fusion.2.grad_ref.refs_4_), channel_id=1, source_target_pairs={{0,2},{2,0},{4,6},{6,4},{8,10},{10,8},{12,14},{14,12},{16,18},{18,... | collective-permute-start | bytes 1572872 | tf_op jit(solution)/shard_map/ppermute | solution.py:588
  120.8 10.4 %collective-permute-start.20 = (bf16[256,1024]{1,0:T(8,128)(2,1)S(1)}, bf16[256,1024]{1,0:T(8,128)(2,1)S(1)}, u32[]{:S(2)}, u32[]{:S(2)}) collective-permute-start(bf16[256,1024]{1,0:T(8,128)(2,1)S(1)} %maximum_select_fusion.1.x_ref.refs_0_), channel_id=1, source_target_pairs={{0,2},{2,0},{4,6},{6,4},{8,10},{10,8},{12,14},{14,12},{16,18},{18,... | collective-permute-start | bytes 1572872 | tf_op jit(solution)/shard_map/ppermute | solution.py:588
  129.7 8.6 %collective-permute-start.19 = (bf16[128,1024]{1,0:T(8,128)(2,1)}, bf16[128,1024]{1,0:T(8,128)(2,1)S(1)}, u32[]{:S(2)}, u32[]{:S(2)}) collective-permute-start(bf16[128,1024]{1,0:T(8,128)(2,1)} %get-tuple-element.66), channel_id=1, source_target_pairs={{0,1},{1,0},{2,3},{3,2},{4,5},{5,4},{6,7},{7,6},{8,9},{9,8},{10,11... | collective-permute-start | bytes 786440 | tf_op jit(solution)/shard_map/ppermute | solution.py:588
  141.6 8.6 %collective-permute-start.24 = (bf16[128,1024]{1,0:T(8,128)(2,1)}, bf16[128,1024]{1,0:T(8,128)(2,1)S(1)}, u32[]{:S(2)}, u32[]{:S(2)}) collective-permute-start(bf16[128,1024]{1,0:T(8,128)(2,1)} %get-tuple-element.71), channel_id=1, source_target_pairs={{0,1},{1,0},{2,3},{3,2},{4,5},{5,4},{6,7},{7,6},{8,9},{9,8},{10,11... | collective-permute-start | bytes 786440 | tf_op jit(solution)/shard_map/ppermute | solution.py:588
  151.4 19.2 %collective-permute-start.37 = (bf16[256,1024]{1,0:T(8,128)(2,1)S(1)}, bf16[256,1024]{1,0:T(8,128)(2,1)S(1)}, u32[]{:S(2)}, u32[]{:S(2)}) collective-permute-start(bf16[256,1024]{1,0:T(8,128)(2,1)S(1)} %maximum_select_fusion.3.dmix_ref.refs_0_), channel_id=1, source_target_pairs={{0,2},{2,0},{4,6},{6,4},{8,10},{10,8},{12,14},{14,12},{16,18},{18,... | collective-permute-start | bytes 1572872 | tf_op jit(solution)/shard_map/ppermute | solution.py:588
  167.6 10.2 %collective-permute-start.26 = (bf16[256,1152]{1,0:T(8,128)(2,1)}, bf16[256,1152]{1,0:T(8,128)(2,1)S(1)}, u32[]{:S(2)}, u32[]{:S(2)}) collective-permute-start(bf16[256,1152]{1,0:T(8,128)(2,1)} %get-tuple-element.73), channel_id=1, source_target_pairs={{0,2},{2,0},{4,6},{6,4},{8,10},{10,8},{12,14},{14,12},{16,18},{18,... | collective-permute-start | bytes 1769480 | tf_op jit(solution)/shard_map/ppermute | solution.py:588
  168.1 9.6 %collective-permute-start.25 = (bf16[256,1024]{1,0:T(8,128)(2,1)S(1)}, bf16[256,1024]{1,0:T(8,128)(2,1)}, u32[]{:S(2)}, u32[]{:S(2)}) collective-permute-start(bf16[256,1024]{1,0:T(8,128)(2,1)S(1)} %copy-done.5), channel_id=1, source_target_pairs={{0,2},{2,0},{4,6},{6,4},{8,10},{10,8},{12,14},{14,12},{16,18},{18,... | collective-permute-start | bytes 1572872 | tf_op jit(solution)/shard_map/ppermute | solution.py:588
  189.0 16.7 %collective-permute-start.27 = (bf16[128,768]{1,0:T(8,128)(2,1)}, bf16[128,768]{1,0:T(8,128)(2,1)S(1)}, u32[]{:S(2)}, u32[]{:S(2)}) collective-permute-start(bf16[128,768]{1,0:T(8,128)(2,1)} %dynamic-slice_convert_fusion), channel_id=1, source_target_pairs={{0,8},{10,2},{8,16},{18,10},{16,24},{26,18},{24,28},{30,26},{28,20... | collective-permute-start | bytes 589832 | tf_op jit(solution)/shard_map/ppermute | solution.py:623
  200.6 12.1 %collective-permute-start.39 = (bf16[128,1024]{1,0:T(8,128)(2,1)}, bf16[128,1024]{1,0:T(8,128)(2,1)}, u32[]{:S(2)}, u32[]{:S(2)}) collective-permute-start(bf16[128,1024]{1,0:T(8,128)(2,1)} %pad_maximum_fusion.4), channel_id=1, source_target_pairs={{0,8},{10,2},{8,16},{18,10},{16,24},{26,18},{24,28},{30,26},{28,20... | collective-permute-start | bytes 786440 | tf_op jit(solution)/shard_map/ppermute | solution.py:623
  203.9 13.9 %collective-permute-start.29 = (bf16[128,1024]{1,0:T(8,128)(2,1)}, bf16[128,1024]{1,0:T(8,128)(2,1)S(1)}, u32[]{:S(2)}, u32[]{:S(2)}) collective-permute-start(bf16[128,1024]{1,0:T(8,128)(2,1)} %get-tuple-element.79), channel_id=1, source_target_pairs={{0,1},{1,0},{2,3},{3,2},{4,5},{5,4},{6,7},{7,6},{8,9},{9,8},{10,11... | collective-permute-start | bytes 786440 | tf_op jit(solution)/shard_map/ppermute | solution.py:588
  211.0 61.1 %collective-permute-start.28 = (bf16[128,1024]{1,0:T(8,128)(2,1)}, bf16[128,1024]{1,0:T(8,128)(2,1)}, u32[]{:S(2)}, u32[]{:S(2)}) collective-permute-start(bf16[128,1024]{1,0:T(8,128)(2,1)} %get-tuple-element.75), channel_id=1, source_target_pairs={{0,1},{1,0},{2,3},{3,2},{4,5},{5,4},{6,7},{7,6},{8,9},{9,8},{10,11... | collective-permute-start | bytes 786440 | tf_op jit(solution)/shard_map/ppermute | solution.py:588
  214.5 10.4 %collective-permute-start.40 = (bf16[128,1024]{1,0:T(8,128)(2,1)S(1)}, bf16[128,1024]{1,0:T(8,128)(2,1)S(1)}, u32[]{:S(2)}, u32[]{:S(2)}) collective-permute-start(bf16[128,1024]{1,0:T(8,128)(2,1)S(1)} %pad_maximum_fusion.5), channel_id=1, source_target_pairs={{0,8},{10,2},{8,16},{18,10},{16,24},{26,18},{24,28},{30,26},{28,20... | collective-permute-start | bytes 786440 | tf_op jit(solution)/shard_map/ppermute | solution.py:623
  233.7 10.3 %collective-permute-start.33 = (bf16[128,768]{1,0:T(8,128)(2,1)S(1)}, bf16[128,768]{1,0:T(8,128)(2,1)S(1)}, u32[]{:S(2)}, u32[]{:S(2)}) collective-permute-start(bf16[128,768]{1,0:T(8,128)(2,1)S(1)} %add_convert_fusion.2), channel_id=1, source_target_pairs={{0,8},{10,2},{8,16},{18,10},{16,24},{26,18},{24,28},{30,26},{28,20... | collective-permute-start | bytes 589832 | tf_op jit(solution)/shard_map/ppermute | solution.py:623
  238.2 11.2 %collective-permute-start.43 = (bf16[128,1024]{1,0:T(8,128)(2,1)S(1)}, bf16[128,1024]{1,0:T(8,128)(2,1)S(1)}, u32[]{:S(2)}, u32[]{:S(2)}) collective-permute-start(bf16[128,1024]{1,0:T(8,128)(2,1)S(1)} %pad_maximum_fusion.8), channel_id=1, source_target_pairs={{0,8},{10,2},{8,16},{18,10},{16,24},{26,18},{24,28},{30,26},{28,20... | collective-permute-start | bytes 786440 | tf_op jit(solution)/shard_map/ppermute | solution.py:623
  244.0 11.2 %collective-permute-start.34 = (bf16[128,768]{1,0:T(8,128)(2,1)S(1)}, bf16[128,768]{1,0:T(8,128)(2,1)S(1)}, u32[]{:S(2)}, u32[]{:S(2)}) collective-permute-start(bf16[128,768]{1,0:T(8,128)(2,1)S(1)} %add_convert_fusion.1), channel_id=1, source_target_pairs={{0,8},{10,2},{8,16},{18,10},{16,24},{26,18},{24,28},{30,26},{28,20... | collective-permute-start | bytes 589832 | tf_op jit(solution)/shard_map/ppermute | solution.py:623
  249.5 9.0 %collective-permute-start.44 = (bf16[128,1024]{1,0:T(8,128)(2,1)S(1)}, bf16[128,1024]{1,0:T(8,128)(2,1)S(1)}, u32[]{:S(2)}, u32[]{:S(2)}) collective-permute-start(bf16[128,1024]{1,0:T(8,128)(2,1)S(1)} %pad_maximum_fusion.9), channel_id=1, source_target_pairs={{0,8},{10,2},{8,16},{18,10},{16,24},{26,18},{24,28},{30,26},{28,20... | collective-permute-start | bytes 786440 | tf_op jit(solution)/shard_map/ppermute | solution.py:623
  256.0 14.6 %collective-permute-start.35 = (bf16[128,768]{1,0:T(8,128)(2,1)}, bf16[128,768]{1,0:T(8,128)(2,1)}, u32[]{:S(2)}, u32[]{:S(2)}) collective-permute-start(bf16[128,768]{1,0:T(8,128)(2,1)} %add_convert_fusion), channel_id=1, source_target_pairs={{0,8},{10,2},{8,16},{18,10},{16,24},{26,18},{24,28},{30,26},{28,20... | collective-permute-start | bytes 589832 | tf_op jit(solution)/shard_map/ppermute | solution.py:623
  (77 other events, 1067.7 us)
Sparse Core Ops, SparseCore 0:
  44.1 68.0 all-gather.1
  168.3 88.5 reduce-scatter.1
where the time goes:
time: 299 us; the launch traced here: 294 us
  waiting for transfers between devices  99.7 us (33%)
  Pallas kernels  67.2 us (22%)
  starting transfers between devices  52.7 us (18%)
  other arithmetic  37.4 us (13%)
  local copies, waits for them, and re-layouts  21.4 us (7%)
  between operations  16 us (5%)
    ppermute x21, waiting for transfers between devices, ring_step(): return lax.ppermute(values, 'dp', pairs)  74.1 us
    pallas_call x10, Pallas kernels, local_call(): pl.pallas_call(kernel, out_shape=[jax.ShapeDtypeStruct(shape, dtype) for...  67.2 us
    ppermute x21, starting transfers between devices, ring_step(): return lax.ppermute(values, 'dp', pairs)  37.3 us
    ppermute x27, waiting for transfers between devices, swap(): return lax.ppermute(values, axis, [(i, i ^ distance) for i in range(count)])  25.5 us
    ppermute x27, starting transfers between devices, swap(): return lax.ppermute(values, axis, [(i, i ^ distance) for i in range(count)])  15.3 us
    sub x7, other arithmetic, adamw(): weight - rate * (fixed_one / (jnp.sqrt(fixed_two) + 1e-08) + decay * weight)  10.2 us
    unnamed x122, local copies, waits for them, and re-layouts  7.55 us
  transfers between devices with their start and end apart: 50, of which 24 were waited for; matrix products, arithmetic and copies ran while one was open for 15% of the time, Pallas kernels for 22%

commit v1 on v0

--- a/solution.py
+++ b/solution.py
@@ -266,7 +266,7 @@
 
 def forward_kernel(
     tidx_ref, lens_ref, p_ref, heads_ref, bc_ref, cos_ref, sin_ref, w_ref,
-    cat_ref, y_ref, mine_ref, theirs_ref, keep_ref, give_ref,
+    cat_ref, y_ref, mix_ref, mix_low_ref, keep_ref, give_ref,
 ):
     parts = mixer_parts(tidx_ref, lens_ref, p_ref, heads_ref, bc_ref)
     for i in range(WIDTH // LANES):
@@ -289,7 +289,8 @@
         a = WIDTH + i * LANES
         cat_ref[:, a : a + LANES] = out.astype(cat_ref.dtype)
     cat = cat_ref[...]
-    split_rows(dot_t(cat, w_ref[:, p_ref.shape[1] :]), tidx_ref[0], mine_ref, theirs_ref)
+    mix_ref[...] = dot_t(cat, w_ref[:, p_ref.shape[1] :])
+    mix_low_ref[...] = mix_ref[...].astype(mix_low_ref.dtype)
     half = cat.shape[1] // 2
     split_columns(cat[:, :half], cat[:, half:], tidx_ref[1], keep_ref, give_ref)
 
@@ -424,8 +425,8 @@
     outs = [
         ((length, width), jnp.bfloat16),
         ((length, WIDTH), jnp.float32),
-        ((length // 2, weight.shape[0]), jnp.float32),
-        ((length // 2, weight.shape[0]), jnp.bfloat16),
+        ((length, weight.shape[0]), jnp.float32),
+        ((length, weight.shape[0]), jnp.bfloat16),
         ((length, width // 2), jnp.bfloat16),
         ((length, width // 2), jnp.bfloat16),
     ]
@@ -435,7 +436,7 @@
     )
 
 
-def mixer_backward(projected, consts, outputs, grad, weight):
+def mixer_backward(projected, consts, outputs, grad, weight, *after):
     length, width = projected.shape
     outs = [
         ((length, width), jnp.bfloat16),
@@ -445,18 +446,19 @@
         ((length, width // 2), jnp.bfloat16),
     ]
     scalars, arrays = consts
-    grad_proj, heads, bc, keep, give = local_call(backward_kernel, outs, "mixer_backward", 2)(
-        *scalars, projected, *arrays, outputs, grad, weight
-    )
+    kernel = lambda *refs: backward_kernel(*refs[:10], *refs[10 + len(after) :])
+    grad_proj, heads, bc, keep, give = local_call(
+        kernel, outs, "mixer_backward", 2, len(after)
+    )(*scalars, projected, *arrays, outputs, grad, weight, *after)
     return grad_proj, heads[:HEADS, : BIAS_COL + 1], bc, keep, give
 
 
 def feed_kernel(
     where_ref, x_ref, grad_ref, w_ref,
-    act_ref, dgu_ref, mine_ref, theirs_ref, keep_ref, give_ref, act_keep_ref, act_give_ref,
+    act_ref, dgu_ref, dx_ref, dx_low_ref, keep_ref, give_ref, act_keep_ref, act_give_ref,
 ):
     units = act_ref.shape[1]
-    tidx, core = where_ref[0], where_ref[1]
+    core = where_ref[1]
     gate_up = dot(x_ref[...], w_ref[:, : 2 * units])
     gate, upper = gate_up[:, :units], gate_up[:, units:]
     sig = jax.nn.sigmoid(gate)
@@ -470,7 +472,8 @@
     dgu_ref[:, :units] = dgate
     dgu_ref[:, units:] = dupper
     split_columns(dgate, dupper, core, keep_ref, give_ref)
-    split_rows(dot_t(dgu_ref[...], w_ref[:, : 2 * units]), tidx, mine_ref, theirs_ref)
+    dx_ref[...] = dot_t(dgu_ref[...], w_ref[:, : 2 * units])
+    dx_low_ref[...] = dx_ref[...].astype(dx_low_ref.dtype)
 
 
 def feed_forward_back(where, values, grad, weight, units):
@@ -479,8 +482,8 @@
     outs = [
         ((length, units), low),
         ((length, 2 * units), low),
-        ((length // 2, width), jnp.float32),
-        ((length // 2, width), low),
+        ((length, width), jnp.float32),
+        ((length, width), low),
         ((length, units), low),
         ((length, units), low),
         ((length, units // 2), low),
@@ -489,22 +492,35 @@
     return local_call(feed_kernel, outs, "feed_forward_back", 1)(where, values, grad, weight)
 
 
-def middle_back(mine, taken, middle, gain, out_grad, *after):
+def middle_forward(resid, mix, taken, gain):
+    def kernel(resid_ref, mix_ref, taken_ref, gain_ref, middle_ref, normed_ref):
+        middle = resid_ref[...] + mix_ref[...] + taken_ref[...].astype(jnp.float32)
+        middle_ref[...] = middle
+        normed_ref[...] = scaled_norm(middle, gain_ref[...]).astype(normed_ref.dtype)
+
+    outs = [(resid.shape, jnp.float32), (resid.shape, jnp.bfloat16)]
+    return local_call(kernel, outs, "middle_forward")(resid, mix, taken, gain[None, :])
+
+
+def middle_back(where, partial, taken, middle, gain, out_grad, *after):
     low = jnp.bfloat16
-
-    def kernel(mine_ref, taken_ref, middle_ref, gain_ref, out_ref, *refs):
+    rows, width = middle.shape
+
+    def kernel(where_ref, part_ref, taken_ref, middle_ref, gain_ref, out_ref, *refs):
         grad_ref, low_ref, gain_grad_ref = refs[len(after) :]
-        grad = mine_ref[...] + taken_ref[...].astype(jnp.float32)
+        first = where_ref[0] == 0
+        grad = part_ref[...] + taken_ref[...].astype(jnp.float32)
         values = middle_ref[...]
         total = out_ref[...] + norm_back(values, gain_ref[...], grad)
-        grad_ref[...] = total
+        grad_ref[...] = jnp.where(first, total[: rows // 2], total[rows // 2 :])
         low_ref[...] = total.astype(low)
-        gain_grad_ref[...] = jnp.sum(grad * values * norm_scale(values), axis=0, keepdims=True)
-
-    shape = middle.shape
-    outs = [(shape, jnp.float32), (shape, low), ((1, shape[1]), jnp.float32)]
-    return local_call(kernel, outs, "middle_back", 0, len(after))(
-        mine, taken, middle, gain[None, :], out_grad, *after
+        share = grad * values * norm_scale(values)
+        share = jnp.where(first, share[: rows // 2], share[rows // 2 :])
+        gain_grad_ref[...] = jnp.sum(share, axis=0, keepdims=True)
+
+    outs = [((rows // 2, width), jnp.float32), ((rows, width), low), ((1, width), jnp.float32)]
+    return local_call(kernel, outs, "middle_back", 1, len(after))(
+        where, partial, taken, middle, gain[None, :], out_grad, *after
     )
 
 
@@ -655,34 +671,53 @@
     return own + other, jnp.stack(blocks).astype(jnp.int32), own
 
 
-def ring_reduce(chains, place, core, rider, last):
+def chunk_grad(chips, step, chain, came, rider, dtype):
+    width = sum(b - a for _, a, b in chain)
+    rows = chain[0][0][0].shape[1] // RING_CHIPS
+    flat = [value for side, _, _ in chain for value in side]
+    flat += [value for value in (came, rider) if value is not None]
+    full = width
+    if rider is not None:
+        full = width + rider.shape[1]
+    elif came is not None and dtype == jnp.bfloat16:
+        full = came.shape[1]
+
+    def kernel(chips_ref, *refs):
+        out_ref = refs[-1]
+        start = pl.multiple_of(chips_ref[step - 1] * rows, rows)
+        mine = pl.ds(start, rows)
+        at, last = 0, 4 * len(chain)
+        for i, (_, a, b) in enumerate(chain):
+            x, y, other_x, other_y = refs[4 * i : 4 * i + 4]
+            part = cross(x[:, mine], y[:, a:b]) + cross(other_x[:, mine], other_y[:, a:b])
+            if came is not None:
+                part = part + refs[last][:, at : at + b - a].astype(jnp.float32)
+            out_ref[:, at : at + b - a] = part.astype(out_ref.dtype)
+            at += b - a
+        if rider is not None:
+            out_ref[:, width:] = refs[last][...]
+        elif full > width:
+            out_ref[:, width:] = refs[last][:, width:]
+
+    return local_call(kernel, [((rows, full), dtype)], "chunk_grad", 1)(chips, *flat)[0]
+
+
+def ring_reduce(chains, place, core, rider):
     way = 1 - 2 * core
+    chips = jnp.stack([ring_chip(place - way * k) for k in range(1, RING_CHIPS + 1)])
+    chips = chips.astype(jnp.int32)
     sums = [None] * len(chains)
     riders = [rider]
-    for step in range(1, RING_CHIPS + 1):
-        chip = ring_chip(place - way * step)
+    for step in range(1, RING_CHIPS):
         for i, chain in enumerate(chains):
-            if step == RING_CHIPS and i == 0:
-                sums[0], last = lax.optimization_barrier((sums[0], last))
-            parts = []
-            for grad, a, b in chain:
-                rows = grad.shape[0] // RING_CHIPS
-                parts.append(lax.dynamic_slice(grad, (chip * rows, a), (rows, b - a)))
-            part = parts[0] if len(parts) == 1 else jnp.concatenate(parts, axis=1)
-            if step > 1:
-                part = part + sums[i].astype(jnp.float32)
-            if step < RING_CHIPS:
-                part = part.astype(jnp.bfloat16)
-                if i == 1:
-                    width = part.shape[1]
-                    part = ring_step(jnp.concatenate([part, riders[-1]], axis=1))
-                    riders.append(part[:, width:])
-                    part = part[:, :width]
-                else:
-                    part = ring_step(part)
-            sums[i] = part
+            riding = rider if step == 1 and i == 1 else None
+            part = chunk_grad(chips, step, chain, sums[i], riding, jnp.bfloat16)
+            sums[i] = ring_step(part)
+        riders.append(sums[1][:, -LANES:])
         if step == 1:
             first = sums[0]
+    for i, chain in enumerate(chains):
+        sums[i] = chunk_grad(chips, RING_CHIPS, chain, sums[i], None, jnp.float32)
     stack = jnp.stack(riders)
     total = 0.0
     for p in range(RING_CHIPS):
@@ -690,7 +725,7 @@
             stack, (way * (place - p)) % RING_CHIPS, axis=0, keepdims=False
         )
         total = total + taken.astype(jnp.float32)
-    return jnp.concatenate(sums, axis=1), total, first, last
+    return jnp.concatenate(sums, axis=1), total, first
 
 
 def both_cores(model_side, keep, give):
@@ -778,7 +813,8 @@
     gain_one, gain_two = shared_params[:D], shared_params[D : 2 * D]
     resid_all = gather_rows(residual, tidx)
     first_all = scaled_norm(resid_all, gain_one).astype(low)
-    grad_feed = gather_rows(out_grad.astype(low), tidx)
+    out_all = gather_rows(out_grad, tidx)
+    grad_feed = out_all.astype(low)
     if ring:
         pieces, blocks, own = ring_gather(first_shard, place, core)
         first_w, projected = place_rows(pieces, blocks, first_all, first_cols)
@@ -788,15 +824,14 @@
         projected = dot(first_all, first_w[:, :first_cols]).astype(low)
     rest_w = lax.all_gather(rest_shard, "dp", axis=0, tiled=True)
     merge_w = first_w[:, first_cols:]
-    joined_low, outputs, mine, theirs, joined_keep, joined_give = mixer_forward(
+    joined_low, outputs, mix, mix_low, joined_keep, joined_give = mixer_forward(
         projected, consts, first_w
     )
-    middle = residual + mine + swap(theirs, "tensor", 1).astype(jnp.float32)
-    second_all = gather_rows(scaled_norm(middle, gain_two).astype(low), tidx)
-    activ_low, grad_gu, mine, theirs, gu_keep, gu_give, act_keep, act_give = feed_forward_back(
+    middle, second_all = middle_forward(resid_all, mix, swap(mix_low, "tensor", 1), gain_two)
+    activ_low, grad_gu, dx, dx_low, gu_keep, gu_give, act_keep, act_give = feed_forward_back(
         where, second_all, grad_feed, rest_w, units
     )
-    taken = swap(theirs, "tensor", 1)
+    taken = swap(dx_low, "tensor", 1)
     waits = []
     if ring:
         rest_grad = weight_grads(
@@ -814,20 +849,17 @@
             tiled=True,
         )
         waits = [rest_grad]
-    grad_middle, grad_low, gain_two_grad = middle_back(
-        mine, taken, middle, gain_two, out_grad, *waits
-    )
-    grad_mixed = gather_rows(grad_low, tidx)
-    grad_proj, head_grad, conv_grad, proj_keep, proj_give = mixer_backward(
-        projected, consts, outputs, grad_mixed, first_w
+    grad_middle, grad_mixed, gain_two_grad = middle_back(
+        where, dx, taken, middle, gain_two, out_all, *waits
     )
     waits = []
     if ring:
-        first_grad = weight_grads([both_cores(first_all, proj_keep, proj_give)], jnp.float32)
-        waits = [first_grad]
-    mine_first, theirs_first, gain_one_grad = first_back(
-        where, grad_proj, first_w, resid_all, *waits
-    )
+        other_first, other_joined = swap(first_all, "dp", 1), swap(joined_give, "dp", 1)
+        waits = [other_first, other_joined]
+    grad_proj, head_grad, conv_grad, proj_keep, proj_give = mixer_backward(
+        projected, consts, outputs, grad_mixed, first_w, *waits
+    )
+    mine_first, theirs_first, gain_one_grad = first_back(where, grad_proj, first_w, resid_all)
     gain_one_grad, gain_two_grad = gain_one_grad.reshape(-1), gain_two_grad.reshape(-1)
     waits = []
     shared_part = jnp.concatenate([gain_one_grad, gain_two_grad, conv_grad.reshape(-1)])
@@ -838,17 +870,15 @@
         down_sum = join_halves(rest_halves, units, rest_sum.shape[1]).T
         hidden_new = adamw(hidden_weight, hidden_first, hidden_second, hidden_sum, 0.02, 0.1)
         down_new = adamw(down_weight, down_first, down_second, down_sum, 0.02, 0.1)
-        merge_grad = weight_grads([both_cores(grad_mixed, joined_keep, joined_give)], jnp.float32)
-        a = first_cols // CORES
-        cut = (a + merge_grad.shape[1]) // 2 // 128 * 128
-        chains = [
-            [(first_grad, 0, cut)],
-            [(first_grad, cut, a), (merge_grad, 0, merge_grad.shape[1])],
-        ]
+        first_sides = (first_all, proj_keep, other_first, swap(proj_give, "dp", 1))
+        merge_sides = (grad_mixed, joined_keep, swap(grad_mixed, "dp", 1), other_joined)
+        a, b = first_cols // CORES, joined_keep.shape[1]
+        cut = (a + b) // 2 // 128 * 128
+        chains = [[(first_sides, 0, cut)], [(first_sides, cut, a), (merge_sides, 0, b)]]
         rows = D // RING_CHIPS
         rider = jnp.pad(small.astype(low), (0, rows * LANES - small.shape[0]))
-        first_sum, small_sum, mark, (hidden_new, down_new) = ring_reduce(
-            chains, place, core, rider.reshape(rows, LANES), (hidden_new, down_new)
+        first_sum, small_sum, mark = ring_reduce(
+            chains, place, core, rider.reshape(rows, LANES)
         )
         waits = [mark]
         half = rows // CORES
@@ -895,6 +925,8 @@
     grad_first = mine_first + swap(theirs_first, "tensor", 1).astype(jnp.float32)
     input_grad = grad_middle + norm_back(residual, gain_one, grad_first)
     mine, theirs = feed_out(where, activ_low, rest_w, *waits)
+    rows = middle.shape[0] // 2
+    middle = jnp.where(tidx == 0, middle[:rows], middle[rows:])
     block_out = middle + mine + swap(theirs, "tensor", 1).astype(jnp.float32)
 
     mixer_new = adamw(mixer_weight, mixer_first, mixer_second, mixer_sum, 0.02, 0.1)

time: 299 us -> 330 us (1.10)
  Pallas kernels: 67.2 us -> 109 us
  other arithmetic: 37.4 us -> 26.6 us
  waiting for transfers between devices: 99.7 us -> 93.3 us
  local copies, waits for them, and re-layouts: 21.4 us -> 27.2 us
    pallas_call x10 -> x25, Pallas kernels: 67.2 us -> 109 us  [local_call(): pl.pallas_call(kernel, out_shape=[jax.ShapeDtypeStruct(shape, dtype) for...]
    unnamed x122 -> x148, local copies, waits for them, and re-layouts: 7.55 us -> 20.5 us
    ppermute x21, starting transfers between devices: 37.3 us -> 43.2 us  [ring_step(): return lax.ppermute(values, 'dp', pairs)]
    ppermute x27 -> x25, starting transfers between devices: 15.3 us -> 9.54 us  [swap(): return lax.ppermute(values, axis, [(i, i ^ distance) for i in range(count)])]
    ppermute x27 -> x25, waiting for transfers between devices: 25.5 us -> 20 us  [swap(): return lax.ppermute(values, axis, [(i, i ^ distance) for i in range(count)])]
    dynamic_slice x2 -> x0, local copies, waits for them, and re-layouts: 4.1 us -> none  [ring_reduce(): parts.append(lax.dynamic_slice(grad, (chip * rows, a), (rows, b - a)))]
  transfers between devices with their start and end apart: 50 -> 48, of which waited for: 24 -> 20; matrix products, arithmetic and copies ran while one was open for 15% -> 10% of each run, Pallas kernels for 22% -> 27%
where the time goes in v1:
time: 330 us; the launch traced here: 325 us
  Pallas kernels  109 us (33%)
  waiting for transfers between devices  93.3 us (28%)
  starting transfers between devices  52.8 us (16%)
  local copies, waits for them, and re-layouts  27.2 us (8%)
  other arithmetic  26.6 us (8%)
  between operations  15.5 us (5%)
    pallas_call x25, Pallas kernels, local_call(): pl.pallas_call(kernel, out_shape=[jax.ShapeDtypeStruct(shape, dtype) for...  109 us
    ppermute x21, waiting for transfers between devices, ring_step(): return lax.ppermute(values, 'dp', pairs)  73.3 us
    ppermute x21, starting transfers between devices, ring_step(): return lax.ppermute(values, 'dp', pairs)  43.2 us
    unnamed x148, local copies, waits for them, and re-layouts  20.5 us
    ppermute x25, waiting for transfers between devices, swap(): return lax.ppermute(values, axis, [(i, i ^ distance) for i in range(count)])  20 us
    ppermute x25, starting transfers between devices, swap(): return lax.ppermute(values, axis, [(i, i ^ distance) for i in range(count)])  9.54 us
    sub x7, other arithmetic, adamw(): weight - rate * (fixed_one / (jnp.sqrt(fixed_two) + 1e-08) + decay * weight)  9.44 us
  transfers between devices with their start and end apart: 48, of which 20 were waited for; matrix products, arithmetic and copies ran while one was open for 10% of the time, Pallas kernels for 27%

profile of v1, /device:TPU:0, one launch (start us, length us, event | category | flops | bytes accessed | tf_op | source)
XLA Modules:
  0.0 324.5 jit_solution(5739390921120485914)
XLA Ops:
  13.5 6.1 %collective-permute-done.1.refs_1_ = bf16[64,3328]{1,0:T(8,128)(2,1)} collective-permute-done((bf16[64,3328]{1,0:T(8,128)(2,1)S(1)}, bf16[64,3328]{1,0:T(8,128)(2,1)}, u32[]{:S(2)}, u32[]{:S(2)}) %collective-permute-start.1) | collective-permute-done | bytes 426016 | tf_op jit(solution)/shard_map/ppermute | solution.py:639
  21.7 6.3 %collective-permute-done.2.refs_2_ = bf16[64,3328]{1,0:T(8,128)(2,1)} collective-permute-done((bf16[64,3328]{1,0:T(8,128)(2,1)}, bf16[64,3328]{1,0:T(8,128)(2,1)}, u32[]{:S(2)}, u32[]{:S(2)}) %collective-permute-start.2) | collective-permute-done | bytes 426016 | tf_op jit(solution)/shard_map/ppermute | solution.py:639
  30.2 6.3 %collective-permute-done.3.refs_3_ = bf16[64,3328]{1,0:T(8,128)(2,1)} collective-permute-done((bf16[64,3328]{1,0:T(8,128)(2,1)}, bf16[64,3328]{1,0:T(8,128)(2,1)}, u32[]{:S(2)}, u32[]{:S(2)}) %collective-permute-start.3) | collective-permute-done | bytes 426016 | tf_op jit(solution)/shard_map/ppermute | solution.py:639
  41.4 3.4 %collective-permute-done.4.refs_4_ = bf16[64,3328]{1,0:T(8,128)(2,1)S(1)} collective-permute-done((bf16[64,3328]{1,0:T(8,128)(2,1)}, bf16[64,3328]{1,0:T(8,128)(2,1)S(1)}, u32[]{:S(2)}, u32[]{:S(2)}) %collective-permute-start.4) | collective-permute-done | bytes 426016 | tf_op jit(solution)/shard_map/ppermute | solution.py:639
  57.3 12.4 %collective-permute-done.6.refs_6_ = bf16[64,3328]{1,0:T(8,128)(2,1)S(1)} collective-permute-done((bf16[64,3328]{1,0:T(8,128)(2,1)S(1)}, bf16[64,3328]{1,0:T(8,128)(2,1)S(1)}, u32[]{:S(2)}, u32[]{:S(2)}) %collective-permute-start.6) | collective-permute-done | bytes 426016 | tf_op jit(solution)/shard_map/ppermute | solution.py:639
  69.6 4.8 %collective-permute-start.7 = (bf16[64,3328]{1,0:T(8,128)(2,1)S(1)}, bf16[64,3328]{1,0:T(8,128)(2,1)S(1)}, u32[]{:S(2)}, u32[]{:S(2)}) collective-permute-start(bf16[64,3328]{1,0:T(8,128)(2,1)S(1)} %collective-permute-done.6.refs_6_), channel_id=1, source_target_pairs={{0,8},{10,2},{8,16},{18,10},{16,24},{26,18},{24,28},{30,26},{28,20... | collective-permute-start | bytes 1277960 | tf_op jit(solution)/shard_map/ppermute | solution.py:639
  77.0 3.6 %collective-permute-done.7.refs_7_ = bf16[64,3328]{1,0:T(8,128)(2,1)S(1)} collective-permute-done((bf16[64,3328]{1,0:T(8,128)(2,1)S(1)}, bf16[64,3328]{1,0:T(8,128)(2,1)S(1)}, u32[]{:S(2)}, u32[]{:S(2)}) %collective-permute-start.7) | collective-permute-done | bytes 426016 | tf_op jit(solution)/shard_map/ppermute | solution.py:639
  84.9 6.8 %place_rows.1 = (bf16[1024,3328]{1,0:T(8,128)(2,1)}, bf16[256,2304]{1,0:T(8,128)(2,1)}) custom-call(s32[16]{0:T(128)} %stack.130.block_ref, bf16[64,3328]{1,0:T(8,128)(2,1)} %copy-done.16, bf16[64,3328]{1,0:T(8,128)(2,1)} %collective-permute-done.1.refs_1_, bf16[64,3328]{1,0:T(8,128)(2,1)} %collective-permute-done.2.refs_2_, ...), custom_call_target="tpu_custom_call" | custom-call | tf_op jit(solution)/shard_map/place_rows/pallas_call | solution.py:392
  91.7 9.6 %mixer_forward.1 = (bf16[256,1024]{1,0:T(8,128)(2,1)}, f32[256,768]{1,0:T(8,128)}, f32[256,1024]{1,0:T(8,128)}, bf16[256,1024]{1,0:T(8,128)(2,1)}, bf16[256,512]{1,0:T(8,128)(2,1)}, /*index=5*/bf16[256,512]{1,0:T(8,128)(2,1)}) custom-call(s32[2]{0:T(128)} %pad_add_fusion.tidx_ref.where_ref.refs_0_, s32[4]{0:T(128)} %bitcast.92, ...), custom_call_target="tpu_custom_call" | custom-call | tf_op jit(solution)/shard_map/mixer_forward/pallas_call | solution.py:392
  103.0 12.4 %collective-permute-done.16.taken_ref = bf16[256,1024]{1,0:T(8,128)(2,1)S(1)} collective-permute-done((bf16[256,1024]{1,0:T(8,128)(2,1)}, bf16[256,1024]{1,0:T(8,128)(2,1)S(1)}, u32[]{:S(2)}, u32[]{:S(2)}) %collective-permute-start.16) | collective-permute-done | bytes 524320 | tf_op jit(solution)/shard_map/ppermute | solution.py:604
  119.2 7.8 %feed_forward_back.1 = (bf16[256,1024]{1,0:T(8,128)(2,1)}, bf16[256,2048]{1,0:T(8,128)(2,1)}, f32[256,1024]{1,0:T(8,128)}, bf16[256,1024]{1,0:T(8,128)(2,1)}, bf...) custom-call(s32[2]{0:T(128)} %pad_add_fusion.tidx_ref.where_ref.refs_0, ...), custom_call_target="tpu_custom_call" | custom-call | tf_op jit(solution)/shard_map/feed_forward_back/pallas_call | solution.py:392
  131.5 5.7 %weight_grads.1.refs_0_ = bf16[1024,1536]{1,0:T(8,128)(2,1)} custom-call(bf16[256,1024]{1,0:T(8,128)(2,1)} %get-tuple-element.58.x_ref.refs_0_, bf16[256,1024]{1,0:T(8,128)(2,1)} %get-tuple-element.64.refs_1_, bf16[256,1024]{1,0:T(8,128)(2,1)} %copy-done.28, bf16[256,1024]{1,0:T(8,128)(2,1)} %copy-done.29, bf16[256,1024]{1,0:T(8,128)(2,1)} %copy-done.9, ...), custom_call_target="tpu_custom_call" | custom-call | tf_op jit(solution)/shard_map/weight_grads/pallas_call | solution.py:392
  137.2 4.4 %collective-permute-done.18.taken_ref = bf16[256,1024]{1,0:T(8,128)(2,1)S(1)} collective-permute-done((bf16[256,1024]{1,0:T(8,128)(2,1)}, bf16[256,1024]{1,0:T(8,128)(2,1)S(1)}, u32[]{:S(2)}, u32[]{:S(2)}) %collective-permute-start.18) | collective-permute-done | bytes 524320 | tf_op jit(solution)/shard_map/ppermute | solution.py:604
  142.4 3.5 %middle_back.1 = (f32[128,1024]{1,0:T(8,128)}, bf16[256,1024]{1,0:T(8,128)(2,1)}, f32[1,1024]{1,0:T(1,128)}) custom-call(s32[2]{0:T(128)} %pad_add_fusion.tidx_ref.where_ref.refs_0_, f32[256,1024]{1,0:T(8,128)} %get-tuple-element.62.part_ref, bf16[256,1024]{1,0:T(8,128)(2,1)} %copy-done.23, f32[256,1024]{1,0:T(8,128)} %get-tuple-element.57.middle_ref, ...), custom_call_target="tpu_custom_call" | custom-call | tf_op jit(solution)/shard_map/middle_back/pallas_call | solution.py:392
  146.8 15.3 %mixer_backward.1 = (bf16[256,2304]{1,0:T(8,128)(2,1)}, f32[16,384]{1,0:T(8,128)}, f32[5,256]{1,0:T(8,128)}, bf16[256,1152]{1,0:T(8,128)(2,1)}, bf16[256,1152]{1,0:T(8,128)(2,1)}) custom-call(s32[2]{0:T(128)} %pad_add_fusion.tidx_ref.where_ref.refs_0_, s32[4]{0:T(128)} %bitcast.93, bf16[256,2304]{1,0:T(8,128)(2,1)} %get-tuple-element.53.p_ref.refs_2_, ...), custom_call_target="tpu_custom_call" | custom-call | tf_op jit(solution)/shard_map/mixer_backward/pallas_call | solution.py:392
  163.2 6.1 %first_back.1 = (f32[128,1024]{1,0:T(8,128)}, bf16[128,1024]{1,0:T(8,128)(2,1)}, f32[1,1024]{1,0:T(1,128)}) custom-call(s32[2]{0:T(128)} %pad_add_fusion.tidx_ref.where_ref.refs_0_, bf16[256,2304]{1,0:T(8,128)(2,1)} %get-tuple-element.75.dp_ref, bf16[1024,3328]{1,0:T(8,128)(2,1)} %get-tuple-element.54.w_ref.refs_9_, f32[256,1024]{1,0:T(8,128)} %copy-done.6), custom_call_target="tpu_custom_call" | custom-call | tf_op jit(solution)/shard_map/first_back/pallas_call | solution.py:392
  172.0 3.1 chunk_grad.24
  175.1 3.9 %collective-permute-start.36 = (bf16[128,1024]{1,0:T(8,128)(2,1)}, bf16[128,1024]{1,0:T(8,128)(2,1)S(1)}, u32[]{:S(2)}, u32[]{:S(2)}) collective-permute-start(bf16[128,1024]{1,0:T(8,128)(2,1)} %chunk_grad.24), channel_id=1, source_target_pairs={{0,8},{10,2},{8,16},{18,10},{16,24},{26,18},{24,28},{30,26},{28,20... | collective-permute-start | bytes 786440 | tf_op jit(solution)/shard_map/ppermute | solution.py:639
  179.0 4.2 %collective-permute-done.36.refs_8_ = bf16[128,1024]{1,0:T(8,128)(2,1)S(1)} collective-permute-done((bf16[128,1024]{1,0:T(8,128)(2,1)}, bf16[128,1024]{1,0:T(8,128)(2,1)S(1)}, u32[]{:S(2)}, u32[]{:S(2)}) %collective-permute-start.36) | collective-permute-done | bytes 262176 | tf_op jit(solution)/shard_map/ppermute | solution.py:639
  183.9 3.2 chunk_grad.25
  187.1 3.9 %collective-permute-start.37 = (bf16[128,1024]{1,0:T(8,128)(2,1)}, bf16[128,1024]{1,0:T(8,128)(2,1)S(1)}, u32[]{:S(2)}, u32[]{:S(2)}) collective-permute-start(bf16[128,1024]{1,0:T(8,128)(2,1)} %chunk_grad.25), channel_id=1, source_target_pairs={{0,8},{10,2},{8,16},{18,10},{16,24},{26,18},{24,28},{30,26},{28,20... | collective-permute-start | bytes 786440 | tf_op jit(solution)/shard_map/ppermute | solution.py:639
  191.5 3.7 %collective-permute-done.37.refs_8_ = bf16[128,1024]{1,0:T(8,128)(2,1)S(1)} collective-permute-done((bf16[128,1024]{1,0:T(8,128)(2,1)}, bf16[128,1024]{1,0:T(8,128)(2,1)S(1)}, u32[]{:S(2)}, u32[]{:S(2)}) %collective-permute-start.37) | collective-permute-done | bytes 262176 | tf_op jit(solution)/shard_map/ppermute | solution.py:639
  195.9 3.3 %chunk_grad.26 = bf16[128,1024]{1,0:T(8,128)(2,1)} custom-call(s32[8]{0:T(128)} %stack.139.chips_ref, bf16[256,1024]{1,0:T(8,128)(2,1)} %multiply_convert_fusion.refs_16_.refs_0_, bf16[256,1152]{1,0:T(8,128)(2,1)} %get-tuple-element.70.refs_1_, bf16[256,1024]{1,0:T(8,128)(2,1)} %copy-done.1, bf16[256,1152]{1,0:T(8,128)(2,1)} %copy-done.2, ...), custom_call_target="tpu_custom_call" | custom-call | tf_op jit(solution)/shard_map/chunk_grad/pallas_call | solution.py:392
  206.7 10.8 %collective-permute-done.26.refs_0_.refs_4_ = bf16[128,768]{1,0:T(8,128)(2,1)S(1)} collective-permute-done((bf16[128,768]{1,0:T(8,128)(2,1)}, bf16[128,768]{1,0:T(8,128)(2,1)S(1)}, u32[]{:S(2)}, u32[]{:S(2)}) %collective-permute-start.26) | collective-permute-done | bytes 196640 | tf_op jit(solution)/shard_map/ppermute | solution.py:639
  224.1 3.2 chunk_grad.27
  231.2 4.7 %feed_out.1 = (f32[128,1024]{1,0:T(8,128)}, bf16[128,1024]{1,0:T(8,128)(2,1)}) custom-call(s32[2]{0:T(128)} %pad_add_fusion.tidx_ref.where_ref.refs_0_, bf16[256,1024]{1,0:T(8,128)(2,1)} %get-tuple-element.60.act_ref, bf16[1024,3072]{1,0:T(8,128)(2,1)} %all-gather.2.cloned.1.call-done.w_ref, bf16[128,768]{1,0:T(8,128)(2,1)} %copy-done.19), custom_call_target="tpu_custom_call" | custom-call | tf_op jit(solution)/shard_map/feed_out/pallas_call | solution.py:392
  240.3 3.2 chunk_grad.28
  250.5 5.1 %collective-permute-done.31.refs_4_ = bf16[128,768]{1,0:T(8,128)(2,1)S(1)} collective-permute-done((bf16[128,768]{1,0:T(8,128)(2,1)}, bf16[128,768]{1,0:T(8,128)(2,1)S(1)}, u32[]{:S(2)}, u32[]{:S(2)}) %collective-permute-start.31) | collective-permute-done | bytes 196640 | tf_op jit(solution)/shard_map/ppermute | solution.py:639
  259.8 3.2 chunk_grad.29
  272.8 4.0 %collective-permute-done.33.refs_4_ = bf16[128,768]{1,0:T(8,128)(2,1)S(1)} collective-permute-done((bf16[128,768]{1,0:T(8,128)(2,1)}, bf16[128,768]{1,0:T(8,128)(2,1)S(1)}, u32[]{:S(2)}, u32[]{:S(2)}) %collective-permute-start.33) | collective-permute-done | bytes 196640 | tf_op jit(solution)/shard_map/ppermute | solution.py:639
  283.1 3.2 chunk_grad.30
  293.5 3.2 chunk_grad.31
  (309 shorter events, 128.6 us)
Async XLA Ops:
  7.2 112.0 %all-gather.2.cloned.1.call-start = ((), (), s32[]{:S(2)}) async-start(), calls=%async_computation.1 | async-start | bytes 6684672 | tf_op jit(solution)/shard_map/all_gather | solution.py:825
  10.4 9.2 %collective-permute-start.1 = (bf16[64,3328]{1,0:T(8,128)(2,1)S(1)}, bf16[64,3328]{1,0:T(8,128)(2,1)}, u32[]{:S(2)}, u32[]{:S(2)}) collective-permute-start(bf16[64,3328]{1,0:T(8,128)(2,1)S(1)} %concatenate.62.refs_0_), channel_id=1, source_target_pairs={{0,8},{10,2},{8,16},{18,10},{16,24},{26,18},{24,28},{30,26},{28,20... | collective-permute-start | bytes 1277960 | tf_op jit(solution)/shard_map/ppermute | solution.py:639
  19.6 8.4 %collective-permute-start.2 = (bf16[64,3328]{1,0:T(8,128)(2,1)}, bf16[64,3328]{1,0:T(8,128)(2,1)}, u32[]{:S(2)}, u32[]{:S(2)}) collective-permute-start(bf16[64,3328]{1,0:T(8,128)(2,1)} %collective-permute-done.1.refs_1_), channel_id=1, source_target_pairs={{0,8},{10,2},{8,16},{18,10},{16,24},{26,18},{24,28},{30,26},{28,20... | collective-permute-start | bytes 1277960 | tf_op jit(solution)/shard_map/ppermute | solution.py:639
  28.1 8.4 %collective-permute-start.3 = (bf16[64,3328]{1,0:T(8,128)(2,1)}, bf16[64,3328]{1,0:T(8,128)(2,1)}, u32[]{:S(2)}, u32[]{:S(2)}) collective-permute-start(bf16[64,3328]{1,0:T(8,128)(2,1)} %collective-permute-done.2.refs_2_), channel_id=1, source_target_pairs={{0,8},{10,2},{8,16},{18,10},{16,24},{26,18},{24,28},{30,26},{28,20... | collective-permute-start | bytes 1277960 | tf_op jit(solution)/shard_map/ppermute | solution.py:639
  36.5 8.3 %collective-permute-start.4 = (bf16[64,3328]{1,0:T(8,128)(2,1)}, bf16[64,3328]{1,0:T(8,128)(2,1)S(1)}, u32[]{:S(2)}, u32[]{:S(2)}) collective-permute-start(bf16[64,3328]{1,0:T(8,128)(2,1)} %collective-permute-done.3.refs_3_), channel_id=1, source_target_pairs={{0,8},{10,2},{8,16},{18,10},{16,24},{26,18},{24,28},{30,26},{28,20... | collective-permute-start | bytes 1277960 | tf_op jit(solution)/shard_map/ppermute | solution.py:639
  44.9 267.1 %reduce-scatter.2.cloned.1.call-start = ((), (), s32[]{:S(2)}) async-start(), calls=%async_computation.2 | async-start | bytes 3538944 | tf_op jit(solution)/shard_map/reduce_scatter | solution.py:844
  44.9 8.2 %collective-permute-start.5 = (bf16[64,3328]{1,0:T(8,128)(2,1)S(1)}, bf16[64,3328]{1,0:T(8,128)(2,1)S(1)}, u32[]{:S(2)}, u32[]{:S(2)}) collective-permute-start(bf16[64,3328]{1,0:T(8,128)(2,1)S(1)} %collective-permute-done.4.refs_4_), channel_id=1, source_target_pairs={{0,8},{10,2},{8,16},{18,10},{16,24},{26,18},{24,28},{30,26},{28,20... | collective-permute-start | bytes 1277960 | tf_op jit(solution)/shard_map/ppermute | solution.py:639
  47.1 28.8 %collective-permute-start.8 = (bf16[64,3328]{1,0:T(8,128)(2,1)S(1)}, bf16[64,3328]{1,0:T(8,128)(2,1)S(1)}, u32[]{:S(2)}, u32[]{:S(2)}) collective-permute-start(bf16[64,3328]{1,0:T(8,128)(2,1)S(1)} %concatenate.62.refs_0_), channel_id=1, source_target_pairs={{0,2},{2,0},{4,6},{6,4},{8,10},{10,8},{12,14},{14,12},{16,18},{18,... | collective-permute-start | bytes 1277960 | tf_op jit(solution)/shard_map/ppermute | solution.py:604
  47.1 27.9 %collective-permute-start = (f32[128,1024]{1,0:T(8,128)S(1)}, f32[128,1024]{1,0:T(8,128)S(1)}, u32[]{:S(2)}, u32[]{:S(2)}) collective-permute-start(f32[128,1024]{1,0:T(8,128)S(1)} %copy-done.7), channel_id=1, source_target_pairs={{0,1},{1,0},{2,3},{3,2},{4,5},{5,4},{6,7},{7,6},{8,9},{9,8},{10,11... | collective-permute-start | bytes 1572872 | tf_op jit(solution)/shard_map/ppermute | solution.py:604
  53.1 16.5 %collective-permute-start.6 = (bf16[64,3328]{1,0:T(8,128)(2,1)S(1)}, bf16[64,3328]{1,0:T(8,128)(2,1)S(1)}, u32[]{:S(2)}, u32[]{:S(2)}) collective-permute-start(bf16[64,3328]{1,0:T(8,128)(2,1)S(1)} %collective-permute-done.5.refs_5_), channel_id=1, source_target_pairs={{0,8},{10,2},{8,16},{18,10},{16,24},{26,18},{24,28},{30,26},{28,20... | collective-permute-start | bytes 1277960 | tf_op jit(solution)/shard_map/ppermute | solution.py:639
  56.7 19.7 %collective-permute-start.9 = (bf16[64,3328]{1,0:T(8,128)(2,1)}, bf16[64,3328]{1,0:T(8,128)(2,1)S(1)}, u32[]{:S(2)}, u32[]{:S(2)}) collective-permute-start(bf16[64,3328]{1,0:T(8,128)(2,1)} %collective-permute-done.1.refs_1_), channel_id=1, source_target_pairs={{0,2},{2,0},{4,6},{6,4},{8,10},{10,8},{12,14},{14,12},{16,18},{18,... | collective-permute-start | bytes 1277960 | tf_op jit(solution)/shard_map/ppermute | solution.py:604
  56.7 19.8 %collective-permute-start.10 = (bf16[64,3328]{1,0:T(8,128)(2,1)}, bf16[64,3328]{1,0:T(8,128)(2,1)S(1)}, u32[]{:S(2)}, u32[]{:S(2)}) collective-permute-start(bf16[64,3328]{1,0:T(8,128)(2,1)} %collective-permute-done.2.refs_2_), channel_id=1, source_target_pairs={{0,2},{2,0},{4,6},{6,4},{8,10},{10,8},{12,14},{14,12},{16,18},{18,... | collective-permute-start | bytes 1277960 | tf_op jit(solution)/shard_map/ppermute | solution.py:604
  69.6 10.9 %collective-permute-start.7 = (bf16[64,3328]{1,0:T(8,128)(2,1)S(1)}, bf16[64,3328]{1,0:T(8,128)(2,1)S(1)}, u32[]{:S(2)}, u32[]{:S(2)}) collective-permute-start(bf16[64,3328]{1,0:T(8,128)(2,1)S(1)} %collective-permute-done.6.refs_6_), channel_id=1, source_target_pairs={{0,8},{10,2},{8,16},{18,10},{16,24},{26,18},{24,28},{30,26},{28,20... | collective-permute-start | bytes 1277960 | tf_op jit(solution)/shard_map/ppermute | solution.py:639
  80.6 21.2 %collective-permute-start.17 = (f32[128,1024]{1,0:T(8,128)S(1)}, f32[128,1024]{1,0:T(8,128)S(1)}, u32[]{:S(2)}, u32[]{:S(2)}) collective-permute-start(f32[128,1024]{1,0:T(8,128)S(1)} %copy-done.25), channel_id=1, source_target_pairs={{0,1},{1,0},{2,3},{3,2},{4,5},{5,4},{6,7},{7,6},{8,9},{9,8},{10,11... | collective-permute-start | bytes 1572872 | tf_op jit(solution)/shard_map/ppermute | solution.py:604
  101.3 14.2 %collective-permute-start.16 = (bf16[256,1024]{1,0:T(8,128)(2,1)}, bf16[256,1024]{1,0:T(8,128)(2,1)S(1)}, u32[]{:S(2)}, u32[]{:S(2)}) collective-permute-start(bf16[256,1024]{1,0:T(8,128)(2,1)} %get-tuple-element.56), channel_id=1, source_target_pairs={{0,1},{1,0},{2,3},{3,2},{4,5},{5,4},{6,7},{7,6},{8,9},{9,8},{10,11... | collective-permute-start | bytes 1572872 | tf_op jit(solution)/shard_map/ppermute | solution.py:604
  103.0 25.2 %collective-permute-start.21 = (bf16[256,1024]{1,0:T(8,128)(2,1)S(1)}, bf16[256,1024]{1,0:T(8,128)(2,1)S(1)}, u32[]{:S(2)}, u32[]{:S(2)}) collective-permute-start(bf16[256,1024]{1,0:T(8,128)(2,1)S(1)} %get-tuple-element.106.grad_ref.refs_4_), channel_id=1, source_target_pairs={{0,2},{2,0},{4,6},{6,4},{8,10},{10,8},{12,14},{14,12},{16,18},{18,... | collective-permute-start | bytes 1572872 | tf_op jit(solution)/shard_map/ppermute | solution.py:604
  119.2 9.5 %collective-permute-start.19 = (bf16[256,1024]{1,0:T(8,128)(2,1)}, bf16[256,1024]{1,0:T(8,128)(2,1)S(1)}, u32[]{:S(2)}, u32[]{:S(2)}) collective-permute-start(bf16[256,1024]{1,0:T(8,128)(2,1)} %get-tuple-element.58.x_ref.refs_0_), channel_id=1, source_target_pairs={{0,2},{2,0},{4,6},{6,4},{8,10},{10,8},{12,14},{14,12},{16,18},{18,... | collective-permute-start | bytes 1572872 | tf_op jit(solution)/shard_map/ppermute | solution.py:604
  127.5 14.1 %collective-permute-start.18 = (bf16[256,1024]{1,0:T(8,128)(2,1)}, bf16[256,1024]{1,0:T(8,128)(2,1)S(1)}, u32[]{:S(2)}, u32[]{:S(2)}) collective-permute-start(bf16[256,1024]{1,0:T(8,128)(2,1)} %get-tuple-element.63), channel_id=1, source_target_pairs={{0,1},{1,0},{2,3},{3,2},{4,5},{5,4},{6,7},{7,6},{8,9},{9,8},{10,11... | collective-permute-start | bytes 1572872 | tf_op jit(solution)/shard_map/ppermute | solution.py:604
  128.2 17.8 %collective-permute-start.23 = (bf16[256,1024]{1,0:T(8,128)(2,1)S(1)}, bf16[256,1024]{1,0:T(8,128)(2,1)S(1)}, u32[]{:S(2)}, u32[]{:S(2)}) collective-permute-start(bf16[256,1024]{1,0:T(8,128)(2,1)S(1)} %copy-done), channel_id=1, source_target_pairs={{0,2},{2,0},{4,6},{6,4},{8,10},{10,8},{12,14},{14,12},{16,18},{18,... | collective-permute-start | bytes 1572872 | tf_op jit(solution)/shard_map/ppermute | solution.py:604
  128.7 17.2 %collective-permute-start.24 = (bf16[256,512]{1,0:T(8,128)(2,1)}, bf16[256,512]{1,0:T(8,128)(2,1)S(1)}, u32[]{:S(2)}, u32[]{:S(2)}) collective-permute-start(bf16[256,512]{1,0:T(8,128)(2,1)} %get-tuple-element.69), channel_id=1, source_target_pairs={{0,2},{2,0},{4,6},{6,4},{8,10},{10,8},{12,14},{14,12},{16,18},{18,... | collective-permute-start | bytes 786440 | tf_op jit(solution)/shard_map/ppermute | solution.py:604
  162.1 8.8 %collective-permute-start.25 = (bf16[256,1152]{1,0:T(8,128)(2,1)}, bf16[256,1152]{1,0:T(8,128)(2,1)S(1)}, u32[]{:S(2)}, u32[]{:S(2)}) collective-permute-start(bf16[256,1152]{1,0:T(8,128)(2,1)} %get-tuple-element.71), channel_id=1, source_target_pairs={{0,2},{2,0},{4,6},{6,4},{8,10},{10,8},{12,14},{14,12},{16,18},{18,... | collective-permute-start | bytes 1769480 | tf_op jit(solution)/shard_map/ppermute | solution.py:604
  162.1 8.8 %collective-permute-start.35 = (bf16[256,1024]{1,0:T(8,128)(2,1)S(1)}, bf16[256,1024]{1,0:T(8,128)(2,1)S(1)}, u32[]{:S(2)}, u32[]{:S(2)}) collective-permute-start(bf16[256,1024]{1,0:T(8,128)(2,1)S(1)} %copy-done.3), channel_id=1, source_target_pairs={{0,2},{2,0},{4,6},{6,4},{8,10},{10,8},{12,14},{14,12},{16,18},{18,... | collective-permute-start | bytes 1572872 | tf_op jit(solution)/shard_map/ppermute | solution.py:604
  175.1 8.1 %collective-permute-start.36 = (bf16[128,1024]{1,0:T(8,128)(2,1)}, bf16[128,1024]{1,0:T(8,128)(2,1)S(1)}, u32[]{:S(2)}, u32[]{:S(2)}) collective-permute-start(bf16[128,1024]{1,0:T(8,128)(2,1)} %chunk_grad.24), channel_id=1, source_target_pairs={{0,8},{10,2},{8,16},{18,10},{16,24},{26,18},{24,28},{30,26},{28,20... | collective-permute-start | bytes 786440 | tf_op jit(solution)/shard_map/ppermute | solution.py:639
  190.9 10.7 %collective-permute-start.28 = (bf16[128,1024]{1,0:T(8,128)(2,1)S(1)}, bf16[128,1024]{1,0:T(8,128)(2,1)S(1)}, u32[]{:S(2)}, u32[]{:S(2)}) collective-permute-start(bf16[128,1024]{1,0:T(8,128)(2,1)S(1)} %copy-done.70), channel_id=1, source_target_pairs={{0,1},{1,0},{2,3},{3,2},{4,5},{5,4},{6,7},{7,6},{8,9},{9,8},{10,11... | collective-permute-start | bytes 786440 | tf_op jit(solution)/shard_map/ppermute | solution.py:604
  199.1 24.2 %collective-permute-start.38 = (bf16[128,1024]{1,0:T(8,128)(2,1)}, bf16[128,1024]{1,0:T(8,128)(2,1)S(1)}, u32[]{:S(2)}, u32[]{:S(2)}) collective-permute-start(bf16[128,1024]{1,0:T(8,128)(2,1)} %chunk_grad.26), channel_id=1, source_target_pairs={{0,8},{10,2},{8,16},{18,10},{16,24},{26,18},{24,28},{30,26},{28,20... | collective-permute-start | bytes 786440 | tf_op jit(solution)/shard_map/ppermute | solution.py:639
  204.4 13.0 %collective-permute-start.26 = (bf16[128,768]{1,0:T(8,128)(2,1)}, bf16[128,768]{1,0:T(8,128)(2,1)S(1)}, u32[]{:S(2)}, u32[]{:S(2)}) collective-permute-start(bf16[128,768]{1,0:T(8,128)(2,1)} %chunk_grad.16), channel_id=1, source_target_pairs={{0,8},{10,2},{8,16},{18,10},{16,24},{26,18},{24,28},{30,26},{28,20... | collective-permute-start | bytes 589832 | tf_op jit(solution)/shard_map/ppermute | solution.py:639
  220.8 15.1 %collective-permute-start.29 = (bf16[128,768]{1,0:T(8,128)(2,1)}, bf16[128,768]{1,0:T(8,128)(2,1)S(1)}, u32[]{:S(2)}, u32[]{:S(2)}) collective-permute-start(bf16[128,768]{1,0:T(8,128)(2,1)} %chunk_grad.17), channel_id=1, source_target_pairs={{0,8},{10,2},{8,16},{18,10},{16,24},{26,18},{24,28},{30,26},{28,20... | collective-permute-start | bytes 589832 | tf_op jit(solution)/shard_map/ppermute | solution.py:639
  227.3 12.3 %collective-permute-start.39 = (bf16[128,1024]{1,0:T(8,128)(2,1)}, bf16[128,1024]{1,0:T(8,128)(2,1)S(1)}, u32[]{:S(2)}, u32[]{:S(2)}) collective-permute-start(bf16[128,1024]{1,0:T(8,128)(2,1)} %chunk_grad.27), channel_id=1, source_target_pairs={{0,8},{10,2},{8,16},{18,10},{16,24},{26,18},{24,28},{30,26},{28,20... | collective-permute-start | bytes 786440 | tf_op jit(solution)/shard_map/ppermute | solution.py:639
  235.9 63.0 %collective-permute-start.27 = (bf16[128,1024]{1,0:T(8,128)(2,1)}, bf16[128,1024]{1,0:T(8,128)(2,1)S(1)}, u32[]{:S(2)}, u32[]{:S(2)}) collective-permute-start(bf16[128,1024]{1,0:T(8,128)(2,1)} %get-tuple-element.73), channel_id=1, source_target_pairs={{0,1},{1,0},{2,3},{3,2},{4,5},{5,4},{6,7},{7,6},{8,9},{9,8},{10,11... | collective-permute-start | bytes 786440 | tf_op jit(solution)/shard_map/ppermute | solution.py:604
  243.6 15.5 %collective-permute-start.40 = (bf16[128,1024]{1,0:T(8,128)(2,1)}, bf16[128,1024]{1,0:T(8,128)(2,1)S(1)}, u32[]{:S(2)}, u32[]{:S(2)}) collective-permute-start(bf16[128,1024]{1,0:T(8,128)(2,1)} %chunk_grad.28), channel_id=1, source_target_pairs={{0,8},{10,2},{8,16},{18,10},{16,24},{26,18},{24,28},{30,26},{28,20... | collective-permute-start | bytes 786440 | tf_op jit(solution)/shard_map/ppermute | solution.py:639
  263.0 19.4 %collective-permute-start.41 = (bf16[128,1024]{1,0:T(8,128)(2,1)}, bf16[128,1024]{1,0:T(8,128)(2,1)S(1)}, u32[]{:S(2)}, u32[]{:S(2)}) collective-permute-start(bf16[128,1024]{1,0:T(8,128)(2,1)} %chunk_grad.29), channel_id=1, source_target_pairs={{0,8},{10,2},{8,16},{18,10},{16,24},{26,18},{24,28},{30,26},{28,20... | collective-permute-start | bytes 786440 | tf_op jit(solution)/shard_map/ppermute | solution.py:639
  280.1 8.4 %collective-permute-start.34 = (bf16[128,768]{1,0:T(8,128)(2,1)}, bf16[128,768]{1,0:T(8,128)(2,1)S(1)}, u32[]{:S(2)}, u32[]{:S(2)}) collective-permute-start(bf16[128,768]{1,0:T(8,128)(2,1)} %chunk_grad.22), channel_id=1, source_target_pairs={{0,8},{10,2},{8,16},{18,10},{16,24},{26,18},{24,28},{30,26},{28,20... | collective-permute-start | bytes 589832 | tf_op jit(solution)/shard_map/ppermute | solution.py:639
  (88 other events, 815.8 us)
Sparse Core Ops, SparseCore 0:
  45.0 67.9 all-gather.1
  191.4 86.6 reduce-scatter.1

commit v2 on v1

--- a/solution.py
+++ b/solution.py
@@ -554,7 +554,7 @@
     return local_call(kernel, outs, "feed_out", 1, len(after))(where, act, weight, *after)
 
 
-def weight_grads(sides, dtype):
+def weight_grads(sides, dtype, *after):
     width = sum(side[1].shape[1] for side in sides)
     model = sides[0][0].shape[1]
     block = 256
@@ -571,7 +571,9 @@
             a = b
 
     flat = [value for side in sides for value in side]
-    return local_call(kernel, [((model, width), dtype)], "weight_grads")(*flat)[0]
+    return local_call(kernel, [((model, width), dtype)], "weight_grads", 0, len(after))(
+        *flat, *after
+    )[0]
 
 
 def cross(left, right):
@@ -671,53 +673,32 @@
     return own + other, jnp.stack(blocks).astype(jnp.int32), own
 
 
-def chunk_grad(chips, step, chain, came, rider, dtype):
-    width = sum(b - a for _, a, b in chain)
-    rows = chain[0][0][0].shape[1] // RING_CHIPS
-    flat = [value for side, _, _ in chain for value in side]
-    flat += [value for value in (came, rider) if value is not None]
-    full = width
-    if rider is not None:
-        full = width + rider.shape[1]
-    elif came is not None and dtype == jnp.bfloat16:
-        full = came.shape[1]
-
-    def kernel(chips_ref, *refs):
-        out_ref = refs[-1]
-        start = pl.multiple_of(chips_ref[step - 1] * rows, rows)
-        mine = pl.ds(start, rows)
-        at, last = 0, 4 * len(chain)
-        for i, (_, a, b) in enumerate(chain):
-            x, y, other_x, other_y = refs[4 * i : 4 * i + 4]
-            part = cross(x[:, mine], y[:, a:b]) + cross(other_x[:, mine], other_y[:, a:b])
-            if came is not None:
-                part = part + refs[last][:, at : at + b - a].astype(jnp.float32)
-            out_ref[:, at : at + b - a] = part.astype(out_ref.dtype)
-            at += b - a
-        if rider is not None:
-            out_ref[:, width:] = refs[last][...]
-        elif full > width:
-            out_ref[:, width:] = refs[last][:, width:]
-
-    return local_call(kernel, [((rows, full), dtype)], "chunk_grad", 1)(chips, *flat)[0]
-
-
 def ring_reduce(chains, place, core, rider):
     way = 1 - 2 * core
-    chips = jnp.stack([ring_chip(place - way * k) for k in range(1, RING_CHIPS + 1)])
-    chips = chips.astype(jnp.int32)
     sums = [None] * len(chains)
     riders = [rider]
-    for step in range(1, RING_CHIPS):
+    for step in range(1, RING_CHIPS + 1):
+        chip = ring_chip(place - way * step)
         for i, chain in enumerate(chains):
-            riding = rider if step == 1 and i == 1 else None
-            part = chunk_grad(chips, step, chain, sums[i], riding, jnp.bfloat16)
-            sums[i] = ring_step(part)
-        riders.append(sums[1][:, -LANES:])
+            parts = []
+            for grad, a, b in chain:
+                rows = grad.shape[0] // RING_CHIPS
+                parts.append(lax.dynamic_slice(grad, (chip * rows, a), (rows, b - a)))
+            part = parts[0] if len(parts) == 1 else jnp.concatenate(parts, axis=1)
+            if step > 1:
+                part = part.astype(jnp.float32) + sums[i].astype(jnp.float32)
+            if step < RING_CHIPS:
+                part = part.astype(jnp.bfloat16)
+                if i == 1:
+                    width = part.shape[1]
+                    part = ring_step(jnp.concatenate([part, riders[-1]], axis=1))
+                    riders.append(part[:, width:])
+                    part = part[:, :width]
+                else:
+                    part = ring_step(part)
+            sums[i] = part
         if step == 1:
             first = sums[0]
-    for i, chain in enumerate(chains):
-        sums[i] = chunk_grad(chips, RING_CHIPS, chain, sums[i], None, jnp.float32)
     stack = jnp.stack(riders)
     total = 0.0
     for p in range(RING_CHIPS):
@@ -874,7 +855,9 @@
         merge_sides = (grad_mixed, joined_keep, swap(grad_mixed, "dp", 1), other_joined)
         a, b = first_cols // CORES, joined_keep.shape[1]
         cut = (a + b) // 2 // 128 * 128
-        chains = [[(first_sides, 0, cut)], [(first_sides, cut, a), (merge_sides, 0, b)]]
+        first_grad = weight_grads([first_sides], low)
+        merge_grad = weight_grads([merge_sides], low, first_grad)
+        chains = [[(first_grad, 0, cut)], [(first_grad, cut, a), (merge_grad, 0, b)]]
         rows = D // RING_CHIPS
         rider = jnp.pad(small.astype(low), (0, rows * LANES - small.shape[0]))
         first_sum, small_sum, mark = ring_reduce(

time: 330 us -> 280 us (0.85)
  Pallas kernels: 109 us -> 70.3 us
  local copies, waits for them, and re-layouts: 27.2 us -> 16.4 us
  starting transfers between devices: 52.8 us -> 61.8 us
  waiting for transfers between devices: 93.3 us -> 85.7 us
    pallas_call x25 -> x11, Pallas kernels: 109 us -> 70.3 us  [local_call(): pl.pallas_call(kernel, out_shape=[jax.ShapeDtypeStruct(shape, dtype) for...]
    ppermute x21, waiting for transfers between devices: 73.3 us -> 58.9 us  [ring_step(): return lax.ppermute(values, 'dp', pairs)]
    unnamed x148 -> x130, local copies, waits for them, and re-layouts: 20.5 us -> 8.12 us
    ppermute x21, starting transfers between devices: 43.2 us -> 51.5 us  [ring_step(): return lax.ppermute(values, 'dp', pairs)]
    ppermute x25, waiting for transfers between devices: 20 us -> 26.8 us  [swap(): return lax.ppermute(values, axis, [(i, i ^ distance) for i in range(count)])]
    dynamic_slice x0 -> x3, local copies, waits for them, and re-layouts: none -> 3.67 us  [ring_reduce(): parts.append(lax.dynamic_slice(grad, (chip * rows, a), (rows, b - a)))]
  transfers between devices with their start and end apart: 48 -> 48, of which waited for: 20 -> 21; matrix products, arithmetic and copies ran while one was open for 10% -> 10% of each run, Pallas kernels for 27% -> 25%
where the time goes in v2:
time: 280 us; the launch traced here: 276 us
  waiting for transfers between devices  85.7 us (31%)
  Pallas kernels  70.3 us (25%)
  starting transfers between devices  61.8 us (22%)
  other arithmetic  26.1 us (9%)
  local copies, waits for them, and re-layouts  16.4 us (6%)
  between operations  15.8 us (6%)
    pallas_call x11, Pallas kernels, local_call(): pl.pallas_call(kernel, out_shape=[jax.ShapeDtypeStruct(shape, dtype) for...  70.3 us
    ppermute x21, waiting for transfers between devices, ring_step(): return lax.ppermute(values, 'dp', pairs)  58.9 us
    ppermute x21, starting transfers between devices, ring_step(): return lax.ppermute(values, 'dp', pairs)  51.5 us
    ppermute x25, waiting for transfers between devices, swap(): return lax.ppermute(values, axis, [(i, i ^ distance) for i in range(count)])  26.8 us
    ppermute x25, starting transfers between devices, swap(): return lax.ppermute(values, axis, [(i, i ^ distance) for i in range(count)])  10.3 us
    sub x7, other arithmetic, adamw(): weight - rate * (fixed_one / (jnp.sqrt(fixed_two) + 1e-08) + decay * weight)  8.72 us
    unnamed x130, local copies, waits for them, and re-layouts  8.12 us
  transfers between devices with their start and end apart: 48, of which 21 were waited for; matrix products, arithmetic and copies ran while one was open for 10% of the time, Pallas kernels for 25%

profile of v2, /device:TPU:0, one launch (start us, length us, event | category | flops | bytes accessed | tf_op | source)
XLA Modules:
  0.0 276.1 jit_solution(7341945917107863775)
XLA Ops:
  10.4 3.1 %collective-permute-start.1 = (bf16[64,3328]{1,0:T(8,128)(2,1)S(1)}, bf16[64,3328]{1,0:T(8,128)(2,1)S(1)}, u32[]{:S(2)}, u32[]{:S(2)}) collective-permute-start(bf16[64,3328]{1,0:T(8,128)(2,1)S(1)} %concatenate.104.refs_0_), channel_id=1, source_target_pairs={{0,8},{10,2},{8,16},{18,10},{16,24},{26,18},{24,28},{30,26},{28,20... | collective-permute-start | bytes 1277960 | tf_op jit(solution)/shard_map/ppermute | solution.py:641
  13.5 6.0 %collective-permute-done.1.refs_1_ = bf16[64,3328]{1,0:T(8,128)(2,1)S(1)} collective-permute-done((bf16[64,3328]{1,0:T(8,128)(2,1)S(1)}, bf16[64,3328]{1,0:T(8,128)(2,1)S(1)}, u32[]{:S(2)}, u32[]{:S(2)}) %collective-permute-start.1) | collective-permute-done | bytes 426016 | tf_op jit(solution)/shard_map/ppermute | solution.py:641
  21.6 6.0 %collective-permute-done.2.refs_2_ = bf16[64,3328]{1,0:T(8,128)(2,1)S(1)} collective-permute-done((bf16[64,3328]{1,0:T(8,128)(2,1)S(1)}, bf16[64,3328]{1,0:T(8,128)(2,1)S(1)}, u32[]{:S(2)}, u32[]{:S(2)}) %collective-permute-start.2) | collective-permute-done | bytes 426016 | tf_op jit(solution)/shard_map/ppermute | solution.py:641
  29.8 6.0 %collective-permute-done.3.refs_3_ = bf16[64,3328]{1,0:T(8,128)(2,1)S(1)} collective-permute-done((bf16[64,3328]{1,0:T(8,128)(2,1)S(1)}, bf16[64,3328]{1,0:T(8,128)(2,1)S(1)}, u32[]{:S(2)}, u32[]{:S(2)}) %collective-permute-start.3) | collective-permute-done | bytes 426016 | tf_op jit(solution)/shard_map/ppermute | solution.py:641
  39.7 4.3 %collective-permute-done.4.refs_4_ = bf16[64,3328]{1,0:T(8,128)(2,1)} collective-permute-done((bf16[64,3328]{1,0:T(8,128)(2,1)S(1)}, bf16[64,3328]{1,0:T(8,128)(2,1)}, u32[]{:S(2)}, u32[]{:S(2)}) %collective-permute-start.4) | collective-permute-done | bytes 426016 | tf_op jit(solution)/shard_map/ppermute | solution.py:641
  50.0 2.6 collective-permute-done.5.refs_5_
  56.8 12.8 %collective-permute-done.6.refs_6_ = bf16[64,3328]{1,0:T(8,128)(2,1)S(1)} collective-permute-done((bf16[64,3328]{1,0:T(8,128)(2,1)}, bf16[64,3328]{1,0:T(8,128)(2,1)S(1)}, u32[]{:S(2)}, u32[]{:S(2)}) %collective-permute-start.6) | collective-permute-done | bytes 426016 | tf_op jit(solution)/shard_map/ppermute | solution.py:641
  69.6 4.1 %collective-permute-start.7 = (bf16[64,3328]{1,0:T(8,128)(2,1)S(1)}, bf16[64,3328]{1,0:T(8,128)(2,1)S(1)}, u32[]{:S(2)}, u32[]{:S(2)}) collective-permute-start(bf16[64,3328]{1,0:T(8,128)(2,1)S(1)} %collective-permute-done.6.refs_6_), channel_id=1, source_target_pairs={{0,8},{10,2},{8,16},{18,10},{16,24},{26,18},{24,28},{30,26},{28,20... | collective-permute-start | bytes 1277960 | tf_op jit(solution)/shard_map/ppermute | solution.py:641
  76.2 4.9 %collective-permute-done.7.refs_7_ = bf16[64,3328]{1,0:T(8,128)(2,1)S(1)} collective-permute-done((bf16[64,3328]{1,0:T(8,128)(2,1)S(1)}, bf16[64,3328]{1,0:T(8,128)(2,1)S(1)}, u32[]{:S(2)}, u32[]{:S(2)}) %collective-permute-start.7) | collective-permute-done | bytes 426016 | tf_op jit(solution)/shard_map/ppermute | solution.py:641
  85.5 6.8 %place_rows.1 = (bf16[1024,3328]{1,0:T(8,128)(2,1)}, bf16[256,2304]{1,0:T(8,128)(2,1)}) custom-call(s32[16]{0:T(128)} %stack.103.block_ref, bf16[64,3328]{1,0:T(8,128)(2,1)} %copy-done.10, bf16[64,3328]{1,0:T(8,128)(2,1)} %copy-done.26, bf16[64,3328]{1,0:T(8,128)(2,1)} %copy-done.27, bf16[64,3328]{1,0:T(8,128)(2,1)} %copy-done.28, ...), custom_call_target="tpu_custom_call" | custom-call | tf_op jit(solution)/shard_map/place_rows/pallas_call | solution.py:392
  92.3 9.5 %mixer_forward.1 = (bf16[256,1024]{1,0:T(8,128)(2,1)}, f32[256,768]{1,0:T(8,128)}, f32[256,1024]{1,0:T(8,128)}, bf16[256,1024]{1,0:T(8,128)(2,1)}, bf16[256,512]{1,0:T(8,128)(2,1)}, /*index=5*/bf16[256,512]{1,0:T(8,128)(2,1)}) custom-call(s32[2]{0:T(128)} %pad_add_fusion.tidx_ref.where_ref.refs_0_, s32[4]{0:T(128)} %bitcast.72, ...), custom_call_target="tpu_custom_call" | custom-call | tf_op jit(solution)/shard_map/mixer_forward/pallas_call | solution.py:392
  103.5 12.6 %collective-permute-done.16.taken_ref = bf16[256,1024]{1,0:T(8,128)(2,1)S(1)} collective-permute-done((bf16[256,1024]{1,0:T(8,128)(2,1)}, bf16[256,1024]{1,0:T(8,128)(2,1)S(1)}, u32[]{:S(2)}, u32[]{:S(2)}) %collective-permute-start.16) | collective-permute-done | bytes 524320 | tf_op jit(solution)/shard_map/ppermute | solution.py:606
  116.8 3.0 %middle_forward.1 = (f32[256,1024]{1,0:T(8,128)}, bf16[256,1024]{1,0:T(8,128)(2,1)}) custom-call(f32[256,1024]{1,0:T(8,128)} %copy-done.1, f32[256,1024]{1,0:T(8,128)} %get-tuple-element.55.mix_ref, bf16[256,1024]{1,0:T(8,128)(2,1)} %copy-done.21, f32[1,1024]{1,0:T(1,128)} %bitcast.70), custom_call_target="tpu_custom_call" | custom-call | tf_op jit(solution)/shard_map/middle_forward/pallas_call | solution.py:392
  119.9 7.9 %feed_forward_back.1 = (bf16[256,1024]{1,0:T(8,128)(2,1)}, bf16[256,2048]{1,0:T(8,128)(2,1)}, f32[256,1024]{1,0:T(8,128)}, bf16[256,1024]{1,0:T(8,128)(2,1)}, bf...) custom-call(s32[2]{0:T(128)} %pad_add_fusion.tidx_ref.where_ref.refs_0, ...), custom_call_target="tpu_custom_call" | custom-call | tf_op jit(solution)/shard_map/feed_forward_back/pallas_call | solution.py:392
  132.3 5.7 %weight_grads.3.refs_0_ = bf16[1024,1536]{1,0:T(8,128)(2,1)} custom-call(bf16[256,1024]{1,0:T(8,128)(2,1)} %get-tuple-element.58.x_ref.refs_0_, bf16[256,1024]{1,0:T(8,128)(2,1)} %get-tuple-element.64.refs_1_, bf16[256,1024]{1,0:T(8,128)(2,1)} %collective-permute-done.19.refs_2_, bf16[256,1024]{1,0:T(8,128)(2,1)} %collective-permute-done.20.refs_3_, ...), custom_call_target="tpu_custom_call" | custom-call | tf_op jit(solution)/shard_map/weight_grads/pallas_call | solution.py:392
  138.0 4.3 %collective-permute-done.18.taken_ref = bf16[256,1024]{1,0:T(8,128)(2,1)S(1)} collective-permute-done((bf16[256,1024]{1,0:T(8,128)(2,1)}, bf16[256,1024]{1,0:T(8,128)(2,1)S(1)}, u32[]{:S(2)}, u32[]{:S(2)}) %collective-permute-start.18) | collective-permute-done | bytes 524320 | tf_op jit(solution)/shard_map/ppermute | solution.py:606
  143.1 3.5 %middle_back.1 = (f32[128,1024]{1,0:T(8,128)}, bf16[256,1024]{1,0:T(8,128)(2,1)}, f32[1,1024]{1,0:T(1,128)}) custom-call(s32[2]{0:T(128)} %pad_add_fusion.tidx_ref.where_ref.refs_0_, f32[256,1024]{1,0:T(8,128)} %get-tuple-element.62.part_ref, bf16[256,1024]{1,0:T(8,128)(2,1)} %copy-done.18, f32[256,1024]{1,0:T(8,128)} %get-tuple-element.57.middle_ref, ...), custom_call_target="tpu_custom_call" | custom-call | tf_op jit(solution)/shard_map/middle_back/pallas_call | solution.py:392
  147.5 15.3 %mixer_backward.1 = (bf16[256,2304]{1,0:T(8,128)(2,1)}, f32[16,384]{1,0:T(8,128)}, f32[5,256]{1,0:T(8,128)}, bf16[256,1152]{1,0:T(8,128)(2,1)}, bf16[256,1152]{1,0:T(8,128)(2,1)}) custom-call(s32[2]{0:T(128)} %pad_add_fusion.tidx_ref.where_ref.refs_0_, s32[4]{0:T(128)} %bitcast.73, bf16[256,2304]{1,0:T(8,128)(2,1)} %get-tuple-element.53.p_ref.refs_2_, ...), custom_call_target="tpu_custom_call" | custom-call | tf_op jit(solution)/shard_map/mixer_backward/pallas_call | solution.py:392
  163.3 6.3 %first_back.1 = (f32[128,1024]{1,0:T(8,128)}, bf16[128,1024]{1,0:T(8,128)(2,1)}, f32[1,1024]{1,0:T(1,128)}) custom-call(s32[2]{0:T(128)} %pad_add_fusion.tidx_ref.where_ref.refs_0_, bf16[256,2304]{1,0:T(8,128)(2,1)} %get-tuple-element.75.dp_ref, bf16[1024,3328]{1,0:T(8,128)(2,1)} %get-tuple-element.54.w_ref.refs_9_, f32[256,1024]{1,0:T(8,128)} %copy-done.1), custom_call_target="tpu_custom_call" | custom-call | tf_op jit(solution)/shard_map/first_back/pallas_call | solution.py:392
  171.4 6.5 %collective-permute-done.28 = bf16[128,1024]{1,0:T(8,128)(2,1)S(1)} collective-permute-done((bf16[128,1024]{1,0:T(8,128)(2,1)}, bf16[128,1024]{1,0:T(8,128)(2,1)S(1)}, u32[]{:S(2)}, u32[]{:S(2)}) %collective-permute-start.28) | collective-permute-done | bytes 262176 | tf_op jit(solution)/shard_map/ppermute | solution.py:606
  180.1 4.5 %weight_grads.4.refs_4_ = bf16[1024,1152]{1,0:T(8,128)(2,1)} custom-call(bf16[256,1024]{1,0:T(8,128)(2,1)} %multiply_convert_fusion.refs_16_.refs_0_, bf16[256,1152]{1,0:T(8,128)(2,1)} %get-tuple-element.70.refs_1_, bf16[256,1024]{1,0:T(8,128)(2,1)} %copy-done.8, bf16[256,1152]{1,0:T(8,128)(2,1)} %copy-done.15), custom_call_target="tpu_custom_call" | custom-call | tf_op jit(solution)/shard_map/weight_grads/pallas_call | solution.py:392
  190.0 3.1 %weight_grads.5 = bf16[1024,512]{1,0:T(8,128)(2,1)} custom-call(bf16[256,1024]{1,0:T(8,128)(2,1)} %get-tuple-element.68.refs_8_.refs_0_, bf16[256,512]{1,0:T(8,128)(2,1)} %get-tuple-element.78.refs_1_, bf16[256,1024]{1,0:T(8,128)(2,1)} %copy-done.20, bf16[256,512]{1,0:T(8,128)(2,1)} %copy-done.11, bf16[1024,1152]{1,0:T(8,128)(2,1)} %weight_grads.4.refs_4_), custom_call_target="tpu_custom_call" | custom-call | tf_op jit(solution)/shard_map/weight_grads/pallas_call | solution.py:392
  194.5 4.1 %collective-permute-start.36 = (bf16[128,1024]{1,0:T(8,128)(2,1)S(1)}, bf16[128,1024]{1,0:T(8,128)(2,1)S(1)}, u32[]{:S(2)}, u32[]{:S(2)}) collective-permute-start(bf16[128,1024]{1,0:T(8,128)(2,1)S(1)} %pad_maximum_fusion.4), channel_id=1, source_target_pairs={{0,8},{10,2},{8,16},{18,10},{16,24},{26,18},{24,28},{30,26},{28,20... | collective-permute-start | bytes 786440 | tf_op jit(solution)/shard_map/ppermute | solution.py:641
  200.2 4.7 %feed_out.1 = (f32[128,1024]{1,0:T(8,128)}, bf16[128,1024]{1,0:T(8,128)(2,1)}) custom-call(s32[2]{0:T(128)} %pad_add_fusion.tidx_ref.where_ref.refs_0_, bf16[256,1024]{1,0:T(8,128)(2,1)} %get-tuple-element.60.act_ref, bf16[1024,3072]{1,0:T(8,128)(2,1)} %all-gather.2.cloned.1.call-done.w_ref, bf16[128,768]{1,0:T(8,128)(2,1)} %copy-done.14), custom_call_target="tpu_custom_call" | custom-call | tf_op jit(solution)/shard_map/feed_out/pallas_call | solution.py:392
  208.2 3.9 %collective-permute-start.37 = (bf16[128,1024]{1,0:T(8,128)(2,1)S(1)}, bf16[128,1024]{1,0:T(8,128)(2,1)S(1)}, u32[]{:S(2)}, u32[]{:S(2)}) collective-permute-start(bf16[128,1024]{1,0:T(8,128)(2,1)S(1)} %pad_maximum_fusion.5), channel_id=1, source_target_pairs={{0,8},{10,2},{8,16},{18,10},{16,24},{26,18},{24,28},{30,26},{28,20... | collective-permute-start | bytes 786440 | tf_op jit(solution)/shard_map/ppermute | solution.py:641
  214.5 2.5 collective-permute-start.30
  218.2 2.5 collective-permute-start.38
  224.8 2.5 collective-permute-start.39
  231.3 2.5 collective-permute-start.40
  237.8 2.5 collective-permute-start.41
  244.4 2.5 collective-permute-start.42
  247.0 3.8 %collective-permute-done.42 = bf16[128,1024]{1,0:T(8,128)(2,1)S(1)} collective-permute-done((bf16[128,1024]{1,0:T(8,128)(2,1)S(1)}, bf16[128,1024]{1,0:T(8,128)(2,1)S(1)}, u32[]{:S(2)}, u32[]{:S(2)}) %collective-permute-start.42) | collective-permute-done | bytes 262176 | tf_op jit(solution)/shard_map/ppermute | solution.py:641
  (306 shorter events, 89.7 us)
Async XLA Ops:
  7.2 112.7 %all-gather.2.cloned.1.call-start = ((), (), s32[]{:S(2)}) async-start(), calls=%async_computation.1 | async-start | bytes 6684672 | tf_op jit(solution)/shard_map/all_gather | solution.py:806
  10.4 9.1 %collective-permute-start.1 = (bf16[64,3328]{1,0:T(8,128)(2,1)S(1)}, bf16[64,3328]{1,0:T(8,128)(2,1)S(1)}, u32[]{:S(2)}, u32[]{:S(2)}) collective-permute-start(bf16[64,3328]{1,0:T(8,128)(2,1)S(1)} %concatenate.104.refs_0_), channel_id=1, source_target_pairs={{0,8},{10,2},{8,16},{18,10},{16,24},{26,18},{24,28},{30,26},{28,20... | collective-permute-start | bytes 1277960 | tf_op jit(solution)/shard_map/ppermute | solution.py:641
  19.5 8.1 %collective-permute-start.2 = (bf16[64,3328]{1,0:T(8,128)(2,1)S(1)}, bf16[64,3328]{1,0:T(8,128)(2,1)S(1)}, u32[]{:S(2)}, u32[]{:S(2)}) collective-permute-start(bf16[64,3328]{1,0:T(8,128)(2,1)S(1)} %collective-permute-done.1.refs_1_), channel_id=1, source_target_pairs={{0,8},{10,2},{8,16},{18,10},{16,24},{26,18},{24,28},{30,26},{28,20... | collective-permute-start | bytes 1277960 | tf_op jit(solution)/shard_map/ppermute | solution.py:641
  27.7 8.1 %collective-permute-start.3 = (bf16[64,3328]{1,0:T(8,128)(2,1)S(1)}, bf16[64,3328]{1,0:T(8,128)(2,1)S(1)}, u32[]{:S(2)}, u32[]{:S(2)}) collective-permute-start(bf16[64,3328]{1,0:T(8,128)(2,1)S(1)} %collective-permute-done.2.refs_2_), channel_id=1, source_target_pairs={{0,8},{10,2},{8,16},{18,10},{16,24},{26,18},{24,28},{30,26},{28,20... | collective-permute-start | bytes 1277960 | tf_op jit(solution)/shard_map/ppermute | solution.py:641
  35.8 8.2 %collective-permute-start.4 = (bf16[64,3328]{1,0:T(8,128)(2,1)S(1)}, bf16[64,3328]{1,0:T(8,128)(2,1)}, u32[]{:S(2)}, u32[]{:S(2)}) collective-permute-start(bf16[64,3328]{1,0:T(8,128)(2,1)S(1)} %collective-permute-done.3.refs_3_), channel_id=1, source_target_pairs={{0,8},{10,2},{8,16},{18,10},{16,24},{26,18},{24,28},{30,26},{28,20... | collective-permute-start | bytes 1277960 | tf_op jit(solution)/shard_map/ppermute | solution.py:641
  44.1 219.5 %reduce-scatter.2.cloned.1.call-start = ((), (), s32[]{:S(2)}) async-start(), calls=%async_computation.2 | async-start | bytes 3538944 | tf_op jit(solution)/shard_map/reduce_scatter | solution.py:825
  44.1 8.5 %collective-permute-start.5 = (bf16[64,3328]{1,0:T(8,128)(2,1)}, bf16[64,3328]{1,0:T(8,128)(2,1)}, u32[]{:S(2)}, u32[]{:S(2)}) collective-permute-start(bf16[64,3328]{1,0:T(8,128)(2,1)} %collective-permute-done.4.refs_4_), channel_id=1, source_target_pairs={{0,8},{10,2},{8,16},{18,10},{16,24},{26,18},{24,28},{30,26},{28,20... | collective-permute-start | bytes 1277960 | tf_op jit(solution)/shard_map/ppermute | solution.py:641
  46.3 28.9 %collective-permute-start.8 = (bf16[64,3328]{1,0:T(8,128)(2,1)S(1)}, bf16[64,3328]{1,0:T(8,128)(2,1)}, u32[]{:S(2)}, u32[]{:S(2)}) collective-permute-start(bf16[64,3328]{1,0:T(8,128)(2,1)S(1)} %concatenate.104.refs_0_), channel_id=1, source_target_pairs={{0,2},{2,0},{4,6},{6,4},{8,10},{10,8},{12,14},{14,12},{16,18},{18,... | collective-permute-start | bytes 1277960 | tf_op jit(solution)/shard_map/ppermute | solution.py:606
  46.3 28.0 %collective-permute-start = (f32[128,1024]{1,0:T(8,128)S(1)}, f32[128,1024]{1,0:T(8,128)S(1)}, u32[]{:S(2)}, u32[]{:S(2)}) collective-permute-start(f32[128,1024]{1,0:T(8,128)S(1)} %copy-done.2), channel_id=1, source_target_pairs={{0,1},{1,0},{2,3},{3,2},{4,5},{5,4},{6,7},{7,6},{8,9},{9,8},{10,11... | collective-permute-start | bytes 1572872 | tf_op jit(solution)/shard_map/ppermute | solution.py:606
  52.6 17.0 %collective-permute-start.6 = (bf16[64,3328]{1,0:T(8,128)(2,1)}, bf16[64,3328]{1,0:T(8,128)(2,1)S(1)}, u32[]{:S(2)}, u32[]{:S(2)}) collective-permute-start(bf16[64,3328]{1,0:T(8,128)(2,1)} %collective-permute-done.5.refs_5_), channel_id=1, source_target_pairs={{0,8},{10,2},{8,16},{18,10},{16,24},{26,18},{24,28},{30,26},{28,20... | collective-permute-start | bytes 1277960 | tf_op jit(solution)/shard_map/ppermute | solution.py:641
  56.2 19.5 %collective-permute-start.9 = (bf16[64,3328]{1,0:T(8,128)(2,1)S(1)}, bf16[64,3328]{1,0:T(8,128)(2,1)S(1)}, u32[]{:S(2)}, u32[]{:S(2)}) collective-permute-start(bf16[64,3328]{1,0:T(8,128)(2,1)S(1)} %collective-permute-done.1.refs_1_), channel_id=1, source_target_pairs={{0,2},{2,0},{4,6},{6,4},{8,10},{10,8},{12,14},{14,12},{16,18},{18,... | collective-permute-start | bytes 1277960 | tf_op jit(solution)/shard_map/ppermute | solution.py:606
  56.2 19.6 %collective-permute-start.10 = (bf16[64,3328]{1,0:T(8,128)(2,1)S(1)}, bf16[64,3328]{1,0:T(8,128)(2,1)S(1)}, u32[]{:S(2)}, u32[]{:S(2)}) collective-permute-start(bf16[64,3328]{1,0:T(8,128)(2,1)S(1)} %collective-permute-done.2.refs_2_), channel_id=1, source_target_pairs={{0,2},{2,0},{4,6},{6,4},{8,10},{10,8},{12,14},{14,12},{16,18},{18,... | collective-permute-start | bytes 1277960 | tf_op jit(solution)/shard_map/ppermute | solution.py:606
  69.6 11.5 %collective-permute-start.7 = (bf16[64,3328]{1,0:T(8,128)(2,1)S(1)}, bf16[64,3328]{1,0:T(8,128)(2,1)S(1)}, u32[]{:S(2)}, u32[]{:S(2)}) collective-permute-start(bf16[64,3328]{1,0:T(8,128)(2,1)S(1)} %collective-permute-done.6.refs_6_), channel_id=1, source_target_pairs={{0,8},{10,2},{8,16},{18,10},{16,24},{26,18},{24,28},{30,26},{28,20... | collective-permute-start | bytes 1277960 | tf_op jit(solution)/shard_map/ppermute | solution.py:641
  75.2 8.5 %collective-permute-start.12 = (bf16[64,3328]{1,0:T(8,128)(2,1)}, bf16[64,3328]{1,0:T(8,128)(2,1)S(1)}, u32[]{:S(2)}, u32[]{:S(2)}) collective-permute-start(bf16[64,3328]{1,0:T(8,128)(2,1)} %collective-permute-done.4.refs_4_), channel_id=1, source_target_pairs={{0,2},{2,0},{4,6},{6,4},{8,10},{10,8},{12,14},{14,12},{16,18},{18,... | collective-permute-start | bytes 1277960 | tf_op jit(solution)/shard_map/ppermute | solution.py:606
  75.7 7.9 %collective-permute-start.13 = (bf16[64,3328]{1,0:T(8,128)(2,1)}, bf16[64,3328]{1,0:T(8,128)(2,1)S(1)}, u32[]{:S(2)}, u32[]{:S(2)}) collective-permute-start(bf16[64,3328]{1,0:T(8,128)(2,1)} %collective-permute-done.5.refs_5_), channel_id=1, source_target_pairs={{0,2},{2,0},{4,6},{6,4},{8,10},{10,8},{12,14},{14,12},{16,18},{18,... | collective-permute-start | bytes 1277960 | tf_op jit(solution)/shard_map/ppermute | solution.py:606
  75.8 7.8 %collective-permute-start.14 = (bf16[64,3328]{1,0:T(8,128)(2,1)S(1)}, bf16[64,3328]{1,0:T(8,128)(2,1)S(1)}, u32[]{:S(2)}, u32[]{:S(2)}) collective-permute-start(bf16[64,3328]{1,0:T(8,128)(2,1)S(1)} %collective-permute-done.6.refs_6_), channel_id=1, source_target_pairs={{0,2},{2,0},{4,6},{6,4},{8,10},{10,8},{12,14},{14,12},{16,18},{18,... | collective-permute-start | bytes 1277960 | tf_op jit(solution)/shard_map/ppermute | solution.py:606
  81.2 21.1 %collective-permute-start.17 = (f32[128,1024]{1,0:T(8,128)S(1)}, f32[128,1024]{1,0:T(8,128)S(1)}, u32[]{:S(2)}, u32[]{:S(2)}) collective-permute-start(f32[128,1024]{1,0:T(8,128)S(1)} %copy-done.22), channel_id=1, source_target_pairs={{0,1},{1,0},{2,3},{3,2},{4,5},{5,4},{6,7},{7,6},{8,9},{9,8},{10,11... | collective-permute-start | bytes 1572872 | tf_op jit(solution)/shard_map/ppermute | solution.py:606
  101.8 14.3 %collective-permute-start.16 = (bf16[256,1024]{1,0:T(8,128)(2,1)}, bf16[256,1024]{1,0:T(8,128)(2,1)S(1)}, u32[]{:S(2)}, u32[]{:S(2)}) collective-permute-start(bf16[256,1024]{1,0:T(8,128)(2,1)} %get-tuple-element.56), channel_id=1, source_target_pairs={{0,1},{1,0},{2,3},{3,2},{4,5},{5,4},{6,7},{7,6},{8,9},{9,8},{10,11... | collective-permute-start | bytes 1572872 | tf_op jit(solution)/shard_map/ppermute | solution.py:606
  103.5 25.2 %collective-permute-start.21 = (bf16[256,1024]{1,0:T(8,128)(2,1)S(1)}, bf16[256,1024]{1,0:T(8,128)(2,1)}, u32[]{:S(2)}, u32[]{:S(2)}) collective-permute-start(bf16[256,1024]{1,0:T(8,128)(2,1)S(1)} %get-tuple-element.106.grad_ref.refs_4_), channel_id=1, source_target_pairs={{0,2},{2,0},{4,6},{6,4},{8,10},{10,8},{12,14},{14,12},{16,18},{18,... | collective-permute-start | bytes 1572872 | tf_op jit(solution)/shard_map/ppermute | solution.py:606
  119.8 9.4 %collective-permute-start.19 = (bf16[256,1024]{1,0:T(8,128)(2,1)}, bf16[256,1024]{1,0:T(8,128)(2,1)}, u32[]{:S(2)}, u32[]{:S(2)}) collective-permute-start(bf16[256,1024]{1,0:T(8,128)(2,1)} %get-tuple-element.58.x_ref.refs_0_), channel_id=1, source_target_pairs={{0,2},{2,0},{4,6},{6,4},{8,10},{10,8},{12,14},{14,12},{16,18},{18,... | collective-permute-start | bytes 1572872 | tf_op jit(solution)/shard_map/ppermute | solution.py:606
  128.2 14.1 %collective-permute-start.18 = (bf16[256,1024]{1,0:T(8,128)(2,1)}, bf16[256,1024]{1,0:T(8,128)(2,1)S(1)}, u32[]{:S(2)}, u32[]{:S(2)}) collective-permute-start(bf16[256,1024]{1,0:T(8,128)(2,1)} %get-tuple-element.63), channel_id=1, source_target_pairs={{0,1},{1,0},{2,3},{3,2},{4,5},{5,4},{6,7},{7,6},{8,9},{9,8},{10,11... | collective-permute-start | bytes 1572872 | tf_op jit(solution)/shard_map/ppermute | solution.py:606
  128.7 17.9 %collective-permute-start.23 = (bf16[256,1024]{1,0:T(8,128)(2,1)S(1)}, bf16[256,1024]{1,0:T(8,128)(2,1)S(1)}, u32[]{:S(2)}, u32[]{:S(2)}) collective-permute-start(bf16[256,1024]{1,0:T(8,128)(2,1)S(1)} %copy-done.3), channel_id=1, source_target_pairs={{0,2},{2,0},{4,6},{6,4},{8,10},{10,8},{12,14},{14,12},{16,18},{18,... | collective-permute-start | bytes 1572872 | tf_op jit(solution)/shard_map/ppermute | solution.py:606
  129.2 17.4 %collective-permute-start.24 = (bf16[256,512]{1,0:T(8,128)(2,1)S(1)}, bf16[256,512]{1,0:T(8,128)(2,1)S(1)}, u32[]{:S(2)}, u32[]{:S(2)}) collective-permute-start(bf16[256,512]{1,0:T(8,128)(2,1)S(1)} %copy-done.61), channel_id=1, source_target_pairs={{0,2},{2,0},{4,6},{6,4},{8,10},{10,8},{12,14},{14,12},{16,18},{18,... | collective-permute-start | bytes 786440 | tf_op jit(solution)/shard_map/ppermute | solution.py:606
  146.6 42.6 %collective-permute-start.35 = (bf16[256,1024]{1,0:T(8,128)(2,1)}, bf16[256,1024]{1,0:T(8,128)(2,1)S(1)}, u32[]{:S(2)}, u32[]{:S(2)}) collective-permute-start(bf16[256,1024]{1,0:T(8,128)(2,1)} %get-tuple-element.68.refs_8_.refs_0_), channel_id=1, source_target_pairs={{0,2},{2,0},{4,6},{6,4},{8,10},{10,8},{12,14},{14,12},{16,18},{18,... | collective-permute-start | bytes 1572872 | tf_op jit(solution)/shard_map/ppermute | solution.py:606
  162.8 16.4 %collective-permute-start.25 = (bf16[256,1152]{1,0:T(8,128)(2,1)}, bf16[256,1152]{1,0:T(8,128)(2,1)S(1)}, u32[]{:S(2)}, u32[]{:S(2)}) collective-permute-start(bf16[256,1152]{1,0:T(8,128)(2,1)} %get-tuple-element.71), channel_id=1, source_target_pairs={{0,2},{2,0},{4,6},{6,4},{8,10},{10,8},{12,14},{14,12},{16,18},{18,... | collective-permute-start | bytes 1769480 | tf_op jit(solution)/shard_map/ppermute | solution.py:606
  169.6 8.3 %collective-permute-start.28 = (bf16[128,1024]{1,0:T(8,128)(2,1)}, bf16[128,1024]{1,0:T(8,128)(2,1)S(1)}, u32[]{:S(2)}, u32[]{:S(2)}) collective-permute-start(bf16[128,1024]{1,0:T(8,128)(2,1)} %get-tuple-element.77), channel_id=1, source_target_pairs={{0,1},{1,0},{2,3},{3,2},{4,5},{5,4},{6,7},{7,6},{8,9},{9,8},{10,11... | collective-permute-start | bytes 786440 | tf_op jit(solution)/shard_map/ppermute | solution.py:606
  185.5 14.1 %collective-permute-start.26 = (bf16[128,768]{1,0:T(8,128)(2,1)S(1)}, bf16[128,768]{1,0:T(8,128)(2,1)S(1)}, u32[]{:S(2)}, u32[]{:S(2)}) collective-permute-start(bf16[128,768]{1,0:T(8,128)(2,1)S(1)} %constant_dynamic-slice_fusion.8), channel_id=1, source_target_pairs={{0,8},{10,2},{8,16},{18,10},{16,24},{26,18},{24,28},{30,26},{28,20... | collective-permute-start | bytes 589832 | tf_op jit(solution)/shard_map/ppermute | solution.py:641
  194.5 13.6 %collective-permute-start.36 = (bf16[128,1024]{1,0:T(8,128)(2,1)S(1)}, bf16[128,1024]{1,0:T(8,128)(2,1)S(1)}, u32[]{:S(2)}, u32[]{:S(2)}) collective-permute-start(bf16[128,1024]{1,0:T(8,128)(2,1)S(1)} %pad_maximum_fusion.4), channel_id=1, source_target_pairs={{0,8},{10,2},{8,16},{18,10},{16,24},{26,18},{24,28},{30,26},{28,20... | collective-permute-start | bytes 786440 | tf_op jit(solution)/shard_map/ppermute | solution.py:641
  205.0 46.1 %collective-permute-start.27 = (bf16[128,1024]{1,0:T(8,128)(2,1)}, bf16[128,1024]{1,0:T(8,128)(2,1)S(1)}, u32[]{:S(2)}, u32[]{:S(2)}) collective-permute-start(bf16[128,1024]{1,0:T(8,128)(2,1)} %get-tuple-element.73), channel_id=1, source_target_pairs={{0,1},{1,0},{2,3},{3,2},{4,5},{5,4},{6,7},{7,6},{8,9},{9,8},{10,11... | collective-permute-start | bytes 786440 | tf_op jit(solution)/shard_map/ppermute | solution.py:606
  206.2 8.2 %collective-permute-start.29 = (bf16[128,768]{1,0:T(8,128)(2,1)S(1)}, bf16[128,768]{1,0:T(8,128)(2,1)S(1)}, u32[]{:S(2)}, u32[]{:S(2)}) collective-permute-start(bf16[128,768]{1,0:T(8,128)(2,1)S(1)} %add_convert_fusion.11), channel_id=1, source_target_pairs={{0,8},{10,2},{8,16},{18,10},{16,24},{26,18},{24,28},{30,26},{28,20... | collective-permute-start | bytes 589832 | tf_op jit(solution)/shard_map/ppermute | solution.py:641
  208.2 9.9 %collective-permute-start.37 = (bf16[128,1024]{1,0:T(8,128)(2,1)S(1)}, bf16[128,1024]{1,0:T(8,128)(2,1)S(1)}, u32[]{:S(2)}, u32[]{:S(2)}) collective-permute-start(bf16[128,1024]{1,0:T(8,128)(2,1)S(1)} %pad_maximum_fusion.5), channel_id=1, source_target_pairs={{0,8},{10,2},{8,16},{18,10},{16,24},{26,18},{24,28},{30,26},{28,20... | collective-permute-start | bytes 786440 | tf_op jit(solution)/shard_map/ppermute | solution.py:641
  253.6 7.2 %collective-permute-start.44 = (f32[64,536]{1,0:T(8,128)}, f32[64,536]{1,0:T(8,128)}, u32[]{:S(2)}, u32[]{:S(2)}) collective-permute-start(f32[64,536]{1,0:T(8,128)} %pad_maximum_fusion.12), channel_id=1, source_target_pairs={{0,1},{1,0},{2,3},{3,2},{4,5},{5,4},{6,7},{7,6},{8,9},{9,8},{10,11... | collective-permute-start | bytes 411656 | tf_op jit(solution)/shard_map/ppermute | solution.py:606
  (79 other events, 792.0 us)
Sparse Core Ops, SparseCore 0:
  44.2 67.9 all-gather.1
  138.1 78.8 reduce-scatter.1
